TPU v7x, 32 devices: a whole 2x2x4 slice. The times are simulated.
32 devices in a mesh: depth: 8 (over z, x), tok: 4 (over y, core).
Axes of the slice: x: 2, y: 2, z: 4, core: 2. Of those that a mesh axis runs over, the one named last changes fastest.
Arguments:
- states: bfloat16 [8, 4096, 2048], P('depth', 'tok'), may hold values from -40 to 40
- w_query: bfloat16 [2048, 1024], replicated, may hold values from -0.25 to 0.25
- w_key: bfloat16 [2048, 256], replicated, may hold values from -0.25 to 0.25
- w_value: bfloat16 [2048, 256], replicated, may hold values from -0.125 to 0.125
Outputs:
- window_out: bfloat16 [8, 4096, 1024], P('depth', 'tok')
- depth_out: bfloat16 [4096, 1024], P(('tok', 'depth'))
All inputs are finite; a program needn't handle non-finite values.
Results may differ from a plain program's by a relative error of at most 0.012.
The roundings to bfloat16 on the way count: a program that leaves them out, or rounds other values in their place, can miss the bound.
Values may be sent and summed in bfloat16 or wider, within the bound.
No kernel may reach another device: no remote copies, remote signals or barrier semaphores. Data moves between devices by JAX's collectives and lax.ppermute only.
A program may use at most 192 MiB of HBM per device.

v0:
```python
import jax
import jax.numpy as jnp
from jax import lax
from jax.sharding import PartitionSpec as P

HQ = 8
HK = 2
HD = 128
WINDOW = 256


def from_behind(value, axis, steps):
    count = lax.axis_size(axis)
    first, last = (max(0, -steps), min(count, count - steps))
    return lax.ppermute(value, axis, [(source, source + steps) for source in range(first, last)])


def from_root(block, axis, owner):
    block = jnp.where(lax.axis_index(axis) == owner, block, jnp.zeros_like(block))
    return lax.psum(block, axis)


def project(rows, weight):
    return jnp.dot(rows, weight, preferred_element_type=jnp.float32).astype(jnp.bfloat16)


def band_attend(query, ext_key, ext_value, base):
    rows = query.shape[0]
    length = ext_key.shape[0]
    group = HQ // HK
    q_heads = query.reshape(rows, HK, group, HD)
    k_heads = ext_key.reshape(length, HK, HD)
    v_heads = ext_value.reshape(length, HK, HD)
    scores = jnp.einsum("qkgd,lkd->kgql", q_heads, k_heads, preferred_element_type=jnp.float32)
    scores = scores / jnp.sqrt(jnp.float32(HD))
    qpos = jnp.arange(rows, dtype=jnp.int32)[:, None]
    kidx = jnp.arange(length, dtype=jnp.int32)[None, :]
    allowed = (kidx >= qpos) & (kidx <= qpos + WINDOW) & (base - WINDOW + kidx >= 0)
    scores = jnp.where(allowed, scores, -jnp.inf)
    top = jnp.max(scores, axis=-1, keepdims=True)
    expo = jnp.exp(scores - top)
    weight = (expo / jnp.sum(expo, axis=-1, keepdims=True)).astype(jnp.bfloat16)
    out = jnp.einsum("kgql,lkd->qkgd", weight, v_heads, preferred_element_type=jnp.float32)
    return out.astype(jnp.bfloat16).reshape(rows, HQ * HD)


def depth_attend(final_q, keys, values):
    steps, count = (keys.shape[0], keys.shape[1])
    group = HQ // HK
    q_heads = final_q.reshape(count, HK, group, HD).astype(jnp.float32)
    k_steps = keys.reshape(steps, count, HK, HD).astype(jnp.float32)
    v_steps = values.reshape(steps, count, HK, HD).astype(jnp.float32)
    scores = jnp.einsum("tkgd,stkd->tkgs", q_heads, k_steps) / jnp.sqrt(jnp.float32(HD))
    top = jnp.max(scores, axis=-1, keepdims=True)
    expo = jnp.exp(scores - top)
    weight = expo / jnp.sum(expo, axis=-1, keepdims=True)
    out = jnp.einsum("tkgs,stkd->tkgd", weight, v_steps)
    return out.astype(jnp.bfloat16).reshape(count, HQ * HD)


def body(states, w_query, w_key, w_value):
    local = states[0]
    rows = local.shape[0]
    steps = lax.axis_size("depth")
    here = lax.axis_index("depth")
    shard = lax.axis_index("tok")
    query = project(local, w_query)
    key = project(local, w_key)
    value = project(local, w_value)
    rim_key, rim_value = from_behind((key[rows - WINDOW :], value[rows - WINDOW :]), "tok", 1)
    ext_key = jnp.concatenate([rim_key, key], axis=0)
    ext_value = jnp.concatenate([rim_value, value], axis=0)
    window_out = band_attend(query, ext_key, ext_value, shard * rows)[None]
    part = rows // steps
    keys, values = (
        lax.all_to_all(key[None], "depth", split_axis=1, concat_axis=0, tiled=True),
        lax.all_to_all(value[None], "depth", split_axis=1, concat_axis=0, tiled=True),
    )
    whole_q = from_root(query, "depth", steps - 1)
    final_q = lax.dynamic_slice_in_dim(whole_q, here * part, part, 0)
    depth_out = depth_attend(final_q, keys, values)
    return (window_out, depth_out)


def solution(mesh):
    in_specs = (P("depth", "tok", None), P(), P(), P())
    out_specs = (P("depth", "tok", None), P(("tok", "depth"), None))
    return jax.shard_map(body, mesh=mesh, in_specs=in_specs, out_specs=out_specs, check_vma=False)
```

profile of v0, /device:TPU:16, one launch (start us, length us, event | category | flops | bytes accessed | tf_op | source)
XLA Modules:
  0.0 144.1 jit_solution(9630555021885596426)
XLA Ops:
  7.2 10.1 %broadcast_select_fusion = (bf16[1024,1024]{0,1:T(8,128)(2,1)}, bf16[1024,1024]{0,1:T(8,128)(2,1)}) fusion(pred[]{:T(512)S(6)} %eq.3, bf16[2048,1024]{1,0:T(8,128)(2,1)} %param.5, bf16[1,1024,2048]{2,1,0:T(8,128)(2,1)} %param.4), kind=kOutput, calls=%fused_computation.16 | convolution fusion | flops 4297064448 | bytes 12582913 | tf_op jit(solution)/shard_map/dot_general | solution.py:24
  17.3 3.4 %fusion.18 = bf16[1024,256]{1,0:T(8,128)(2,1)S(1)} fusion(bf16[2048,256]{1,0:T(8,128)(2,1)S(1)} %copy-done, bf16[1,1024,2048]{2,1,0:T(8,128)(2,1)} %param.4), kind=kOutput, calls=%fused_computation.20 | convolution fusion | flops 1074003968 | bytes 5767168 | tf_op jit(solution)/shard_map/dot_general | solution.py:24
  20.8 0.8 copy.70
  22.2 3.9 %reduce.5 = bf16[1024,256]{1,0:T(8,128)(2,1)S(1)} reduce(bf16[1024,1,256]{2,1,0:T(2,128)(2,1)S(1)} %bitcast.52, bf16[]{:T(256)} %broadcast.25), dimensions={1}, to_apply=%bitcast.51.reduce_sub_computation | reduce | bytes 1048578
  26.1 0.9 reshape.64
  27.0 6.1 %all-to-all-start = ((bf16[8,2,16384]{2,1,0:T(2,128)(2,1)}), bf16[8,2,16384]{2,1,0:T(2,128)(2,1)S(1)}, u32[]{:S(2)}, u32[]{:S(2)}) async-start(bf16[8,2,16384]{2,1,0:T(2,128)(2,1)} %reshape.64), calls=%async_computation | async-start | bytes 1048576 | tf_op jit(solution)/shard_map/all_to_all | solution.py:76
  33.8 1.3 collective-permute-start.1
  35.1 3.5 %fusion.15 = bf16[1024,256]{1,0:T(8,128)(2,1)S(1)} fusion(bf16[2048,256]{1,0:T(8,128)(2,1)S(1)} %copy-done.2, bf16[1,1024,2048]{2,1,0:T(8,128)(2,1)} %param.4), kind=kOutput, calls=%fused_computation.19 | convolution fusion | flops 1074003968 | bytes 5767168 | tf_op jit(solution)/shard_map/dot_general | solution.py:24
  38.6 4.3 %collective-permute-start = (bf16[256,256]{1,0:T(8,128)(2,1)S(1)}, bf16[256,256]{1,0:T(8,128)(2,1)S(1)}, u32[]{:S(2)}, u32[]{:S(2)}) collective-permute-start(bf16[256,256]{1,0:T(8,128)(2,1)S(1)} %slice.8), channel_id=1, source_target_pairs={{0,1},{1,2},{2,3},{4,5},{5,6},{6,7},{8,9},{9,10},{10,11},{12,13},{... | collective-permute-start | bytes 393224 | tf_op jit(solution)/shard_map/ppermute | solution.py:15
  43.0 2.6 %fusion.4 = pred[1024,1280]{0,1:T(8,128)(4,1)} fusion(s32[1024]{0:T(1024)S(1)} %iota_add_fusion, pred[1280]{0:T(1024)(128)(4,1)S(1)} %add_compare_fusion), kind=kLoop, calls=%fused_computation.9 | loop fusion | flops 5242880 | bytes 1316096 | tf_op jit(solution)/shard_map/and | solution.py:38
  45.6 0.8 copy.69
  46.4 3.9 %reduce.4 = bf16[1024,256]{1,0:T(8,128)(2,1)S(1)} reduce(bf16[1024,1,256]{2,1,0:T(2,128)(2,1)S(1)} %bitcast.53, bf16[]{:T(256)} %broadcast.25), dimensions={1}, to_apply=%bitcast.50.reduce_sub_computation | reduce | bytes 1048578
  50.3 0.9 reshape.62
  51.4 19.8 %exponential_reduce_fusion = (f32[2,4,1024]{2,1,0:T(4,128)S(1)}, f32[2,4,1024,1280]{2,3,1,0:T(8,128)}) fusion(bf16[1024,2,4,128]{0,3,2,1:T(8,128)(2,1)} %bitcast.60, pred[1024,1280]{0,1:T(8,128)(4,1)} %fusion.4, bf16[1280,2,128,1]{2,1,0,3:T(2,128)(2,1)S(1)} %bitcast.59), kind=kOutput, calls=%fused_computation.4 | convolution fusion | flops 2726298880 | bytes 46039040 | tf_op jit(solution)/shard_map/sub | solution.py:41
  71.2 1.1 copy.45
  72.3 6.0 %all-to-all-start.1 = ((bf16[8,2,16384]{2,1,0:T(2,128)(2,1)}), bf16[8,2,16384]{2,1,0:T(2,128)(2,1)S(1)}, u32[]{:S(2)}, u32[]{:S(2)}) async-start(bf16[8,2,16384]{2,1,0:T(2,128)(2,1)} %reshape.62), calls=%async_computation.1 | async-start | bytes 1048576 | tf_op jit(solution)/shard_map/all_to_all | solution.py:77
  78.3 17.2 %fusion.11 = bf16[2,128,4,1024]{3,1,2,0:T(8,128)(2,1)S(1)} fusion(bf16[1280,2,128,1]{0,2,3,1:T(8,128)(2,1)} %bitcast.58, f32[2,4,1024,1280]{2,3,1,0:T(8,128)} %get-tuple-element.11, f32[2,4,1024]{2,1,0:T(4,128)S(1)} %get-tuple-element.10), kind=kOutput, calls=%fused_computation.17 | convolution fusion | flops 2706374656 | bytes 44728320 | tf_op jit(solution)/shard_map/kgql,lkd->qkgd/dot_general | solution.py:43
  95.5 2.6 %copy.40 = bf16[1,1024,1024]{2,1,0:T(8,128)(2,1)} copy(bf16[1,1024,1024]{1,2,0:T(8,128)(2,1)S(1)} %bitcast.56) | data formatting | bytes 4194304
  98.6 3.1 %bitcast_reduce_fusion = bf16[1024,256]{1,0:T(8,128)(2,1)S(1)} fusion(bf16[1024,1,256]{2,1,0:T(2,128)(2,1)S(1)} %reshape.65), kind=kLoop, calls=%fused_computation.41 | loop fusion | bytes 1048576 | tf_op jit(solution)/shard_map/all_to_all | solution.py:76
  102.6 3.1 %bitcast_reduce_fusion.1 = bf16[1024,256]{1,0:T(8,128)(2,1)S(1)} fusion(bf16[1024,1,256]{2,1,0:T(2,128)(2,1)S(1)} %reshape.63), kind=kLoop, calls=%fused_computation.42 | loop fusion | bytes 1048576 | tf_op jit(solution)/shard_map/all_to_all | solution.py:77
  105.8 26.9 %all-reduce.2.cloned.1.call-done = bf16[1024,1024]{0,1:T(8,128)(2,1)} async-done(((bf16[1024,1024]{0,1:T(8,128)(2,1)}), bf16[1024,1024]{0,1:T(8,128)(2,1)}) %all-reduce.2.cloned.1.call-update) | async-done | bytes 2097168 | tf_op jit(solution)/shard_map/psum | solution.py:20
  132.7 1.0 constant_dynamic-slice_fusion
  135.4 1.0 convolution_convert_fusion
  136.4 0.9 reshape.55
  (27 shorter events, 4.9 us)
Async XLA Ops:
  7.2 10.2 %copy-start = (bf16[2048,256]{1,0:T(8,128)(2,1)S(1)}, bf16[2048,256]{1,0:T(8,128)(2,1)}, u32[]{:S(2)}) copy-start(bf16[2048,256]{1,0:T(8,128)(2,1)} %param.6) | copy-start | bytes 3145732
  7.2 125.5 %all-reduce.2.cloned.1.call-start = ((), (), s32[]{:S(2)}) async-start(), calls=%async_computation.2 | async-start | bytes 4194304 | tf_op jit(solution)/shard_map/psum | solution.py:20
  20.8 14.3 %copy-start.2 = (bf16[2048,256]{1,0:T(8,128)(2,1)S(1)}, bf16[2048,256]{1,0:T(8,128)(2,1)}, u32[]{:S(2)}) copy-start(bf16[2048,256]{1,0:T(8,128)(2,1)} %param.7) | copy-start | bytes 3145732
  27.0 45.3 %all-to-all-start = ((bf16[8,2,16384]{2,1,0:T(2,128)(2,1)}), bf16[8,2,16384]{2,1,0:T(2,128)(2,1)S(1)}, u32[]{:S(2)}, u32[]{:S(2)}) async-start(bf16[8,2,16384]{2,1,0:T(2,128)(2,1)} %reshape.64), calls=%async_computation | async-start | bytes 1048576 | tf_op jit(solution)/shard_map/all_to_all | solution.py:76
  33.8 17.4 %collective-permute-start.1 = (bf16[256,256]{1,0:T(8,128)(2,1)}, bf16[256,256]{1,0:T(8,128)(2,1)S(1)}, u32[]{:S(2)}, u32[]{:S(2)}) collective-permute-start(bf16[256,256]{1,0:T(8,128)(2,1)} %slice.9), channel_id=1, source_target_pairs={{0,1},{1,2},{2,3},{4,5},{5,6},{6,7},{8,9},{9,10},{10,11},{12,13},{... | collective-permute-start | bytes 393224 | tf_op jit(solution)/shard_map/ppermute | solution.py:15
  38.6 32.6 %collective-permute-start = (bf16[256,256]{1,0:T(8,128)(2,1)S(1)}, bf16[256,256]{1,0:T(8,128)(2,1)S(1)}, u32[]{:S(2)}, u32[]{:S(2)}) collective-permute-start(bf16[256,256]{1,0:T(8,128)(2,1)S(1)} %slice.8), channel_id=1, source_target_pairs={{0,1},{1,2},{2,3},{4,5},{5,6},{6,7},{8,9},{9,10},{10,11},{12,13},{... | collective-permute-start | bytes 393224 | tf_op jit(solution)/shard_map/ppermute | solution.py:15
  72.3 29.4 %all-to-all-start.1 = ((bf16[8,2,16384]{2,1,0:T(2,128)(2,1)}), bf16[8,2,16384]{2,1,0:T(2,128)(2,1)S(1)}, u32[]{:S(2)}, u32[]{:S(2)}) async-start(bf16[8,2,16384]{2,1,0:T(2,128)(2,1)} %reshape.62), calls=%async_computation.1 | async-start | bytes 1048576 | tf_op jit(solution)/shard_map/all_to_all | solution.py:77
  135.4 1.9 %copy-start.1 = (bf16[2048,256]{1,0:T(8,128)(2,1)S(1)}, bf16[2048,256]{1,0:T(8,128)(2,1)}, u32[]{:S(2)}) copy-start(bf16[2048,256]{1,0:T(8,128)(2,1)} %param.6) | copy-start | bytes 3145732
Sparse Core Ops, SparseCore 0:
  17.4 115.1 all-reduce.1
where the time goes:
time: 146 us; the launch traced here: 144 us
  matrix products  55.6 us (38%)
  waiting for transfers between devices  26.9 us (18%)
  local copies, waits for them, and re-layouts  18.3 us (13%)
  starting transfers between devices  17.8 us (12%)
  between operations  14.3 us (10%)
  other arithmetic  11.3 us (8%)
    psum x1, waiting for transfers between devices, from_root(): return lax.psum(block, axis)  26.9 us
    sub x1, matrix products, band_attend(): expo = jnp.exp(scores - top)  19.8 us
    dot_general x1, matrix products, band_attend(): jnp.einsum('kgql,lkd->qkgd', weight, v_heads, preferred_element_type=jnp....  17.2 us
    dot_general x3, matrix products, project(): jnp.dot(rows, weight, preferred_element_type=jnp.float32)  17 us
    unnamed x2, other arithmetic  7.74 us
    unnamed x12, local copies, waits for them, and re-layouts  6.35 us
    all_to_all x1, starting transfers between devices, body(): lax.all_to_all(key[None], 'depth', split_axis=1, concat_axis=0, tiled=True)  6.14 us
    all_to_all x1, starting transfers between devices, body(): lax.all_to_all(value[None], 'depth', split_axis=1, concat_axis=0, tiled=T...  5.99 us
  transfers between devices with their start and end apart: 5, of which 1 were waited for; matrix products, arithmetic and copies ran while one was open for 49% of the time, Pallas kernels for 0%

commit v1 on v0

v1 whole, which is shorter than its diff:
```python
import functools
import math

import jax
import jax.numpy as jnp
from jax import lax
from jax.experimental import pallas as pl
from jax.experimental.pallas import tpu as pltpu
from jax.sharding import PartitionSpec as P

HQ = 8
HK = 2
HD = 128
WINDOW = 256
GROUP = HQ // HK
SCALE = 1.0 / math.sqrt(HD)
VMEM_BYTES = 48 * 1024 * 1024


def params(*semantics):
    return pltpu.CompilerParams(
        dimension_semantics=semantics or None, vmem_limit_bytes=VMEM_BYTES
    )


def project_q_kernel(x_ref, w_ref, *out_refs):
    part = out_refs[0].shape[0]
    for index, out_ref in enumerate(out_refs):
        out_ref[...] = jnp.dot(
            x_ref[pl.ds(index * part, part), :],
            w_ref[...],
            preferred_element_type=jnp.float32,
        ).astype(jnp.bfloat16)


def project_q(rows, weight, parts):
    count, depth = rows.shape
    width = weight.shape[1]
    part = count // parts
    return pl.pallas_call(
        project_q_kernel,
        out_shape=[jax.ShapeDtypeStruct((part, width), jnp.bfloat16)] * parts,
        in_specs=[pl.BlockSpec(memory_space=pltpu.VMEM)] * 2,
        out_specs=[pl.BlockSpec(memory_space=pltpu.VMEM)] * parts,
        compiler_params=params(),
        cost_estimate=pl.CostEstimate(
            flops=2 * count * depth * width,
            bytes_accessed=2 * (count * depth + depth * width + count * width),
            transcendentals=0,
        ),
    )(rows, weight)


def project_kv_kernel(x_ref, wk_ref, wv_ref, out_ref):
    width = wk_ref.shape[1]
    x = x_ref[...]
    out_ref[:, :width] = jnp.dot(x, wk_ref[...], preferred_element_type=jnp.float32).astype(jnp.bfloat16)
    out_ref[:, width:] = jnp.dot(x, wv_ref[...], preferred_element_type=jnp.float32).astype(jnp.bfloat16)


def project_kv(rows, w_key, w_value):
    count, depth = rows.shape
    width = w_key.shape[1]
    block = min(count, 256)
    whole = pl.BlockSpec((depth, width), lambda i: (0, 0))
    return pl.pallas_call(
        project_kv_kernel,
        grid=(count // block,),
        out_shape=jax.ShapeDtypeStruct((count, 2 * width), jnp.bfloat16),
        in_specs=[pl.BlockSpec((block, depth), lambda i: (i, 0)), whole, whole],
        out_specs=pl.BlockSpec((block, 2 * width), lambda i: (i, 0)),
        compiler_params=params("arbitrary"),
        cost_estimate=pl.CostEstimate(
            flops=4 * count * depth * width,
            bytes_accessed=2 * (count * depth + 2 * depth * width + 2 * count * width),
            transcendentals=0,
        ),
    )(rows, w_key, w_value)


BAND = 128


def band_kernel(parts, first_ref, *refs):
    q_refs, (kv_ref, rim_ref, out_ref) = refs[:parts], refs[parts:]
    part = q_refs[0].shape[0]
    count, width = kv_ref.shape
    width //= 2
    first = first_ref[0] == 1
    row = lax.broadcasted_iota(jnp.int32, (GROUP * BAND, BAND), 0) % BAND
    column = lax.broadcasted_iota(jnp.int32, (GROUP * BAND, BAND), 1)
    behind = column >= row
    ahead = column <= row
    ones = jnp.ones((BAND, HD), jnp.bfloat16)

    def chunk(index, low, high):
        if index < 0:
            return rim_ref[pl.ds(WINDOW + index * BAND, BAND), low:high]
        return kv_ref[pl.ds(index * BAND, BAND), low:high]

    def queries(index, head):
        start = index * BAND
        pieces = []
        size = min(part, BAND)
        for at in range(start, start + BAND, size):
            pieces.append(q_refs[at // part][pl.ds(at % part, size), head * HD : (head + 1) * HD])
        return pieces

    blocks = WINDOW // BAND + 1
    for index in range(count // BAND):
        for c in range(HK):
            q = jnp.concatenate(
                [piece for h in range(c * GROUP, (c + 1) * GROUP) for piece in queries(index, h)], axis=0
            )
            at = [index + j - (blocks - 1) for j in range(blocks)]
            k = jnp.concatenate([chunk(a, c * HD, (c + 1) * HD) for a in at], axis=0)
            v = jnp.concatenate([chunk(a, width + c * HD, width + (c + 1) * HD) for a in at], axis=0)
            v = jnp.concatenate([v, jnp.concatenate([ones] * blocks, axis=0)], axis=1)
            s = lax.dot_general(q, k, (((1,), (1,)), ((), ())), preferred_element_type=jnp.float32)
            tiles = []
            for j in range(blocks):
                t = s[:, j * BAND : (j + 1) * BAND]
                allowed = None
                if j == 0:
                    allowed = behind
                elif j == blocks - 1:
                    allowed = ahead
                if at[j] < 0:
                    some = jnp.logical_not(first)
                    allowed = some if allowed is None else jnp.logical_and(allowed, some)
                if allowed is not None:
                    t = jnp.where(allowed, t, -jnp.inf)
                tiles.append(t)
            top = functools.reduce(jnp.maximum, tiles)
            top = jnp.max(top, axis=-1, keepdims=True)
            p = jnp.concatenate(
                [jnp.exp2((t - top) * (SCALE * math.log2(math.e))).astype(jnp.bfloat16) for t in tiles], axis=1
            )
            o = jnp.dot(p, v, preferred_element_type=jnp.float32)
            o = (o[:, :HD] / o[:, HD:]).astype(jnp.bfloat16)
            for g in range(GROUP):
                h = c * GROUP + g
                out_ref[pl.ds(index * BAND, BAND), h * HD : (h + 1) * HD] = o[g * BAND : (g + 1) * BAND]


def band_attend(queries, kv, rim, first):
    parts = len(queries)
    count = kv.shape[0]
    width = queries[0].shape[1]
    vmem = pl.BlockSpec(memory_space=pltpu.VMEM)
    return pl.pallas_call(
        functools.partial(band_kernel, parts),
        out_shape=jax.ShapeDtypeStruct((count, width), jnp.bfloat16),
        in_specs=[pl.BlockSpec(memory_space=pltpu.SMEM)] + [vmem] * (parts + 2),
        out_specs=vmem,
        compiler_params=params(),
        cost_estimate=pl.CostEstimate(
            flops=4 * count * width * (WINDOW + BAND),
            bytes_accessed=4 * count * width + 2 * kv.size,
            transcendentals=HQ * count * (WINDOW + BAND),
        ),
    )(first, *queries, kv, rim)


def depth_kernel(q_ref, kv_ref, out_ref):
    steps, count, width = kv_ref.shape
    width //= 2
    chunk = min(count, 32)
    for start in range(0, count, chunk):
        rows = pl.ds(start, chunk)
        for c in range(HK):
            keys = [kv_ref[s, rows, c * HD : (c + 1) * HD].astype(jnp.float32) for s in range(steps)]
            values = [
                kv_ref[s, rows, width + c * HD : width + (c + 1) * HD].astype(jnp.float32) for s in range(steps)
            ]
            for h in range(c * GROUP, (c + 1) * GROUP):
                q = q_ref[rows, h * HD : (h + 1) * HD].astype(jnp.float32)
                scores = [jnp.sum(q * k, axis=-1, keepdims=True) * SCALE for k in keys]
                top = functools.reduce(jnp.maximum, scores)
                expo = [jnp.exp(s - top) for s in scores]
                total = functools.reduce(jnp.add, expo)
                out = functools.reduce(jnp.add, [e * v for e, v in zip(expo, values)])
                out_ref[rows, h * HD : (h + 1) * HD] = (out / total).astype(jnp.bfloat16)


def depth_attend(query, kv):
    vmem = pl.BlockSpec(memory_space=pltpu.VMEM)
    return pl.pallas_call(
        depth_kernel,
        out_shape=jax.ShapeDtypeStruct(query.shape, jnp.bfloat16),
        in_specs=[vmem] * 2,
        out_specs=vmem,
        compiler_params=params(),
        cost_estimate=pl.CostEstimate(
            flops=4 * query.size * kv.shape[0],
            bytes_accessed=2 * (2 * query.size + kv.size),
            transcendentals=query.shape[0] * HQ * kv.shape[0],
        ),
    )(query, kv)


def scatter_last(blocks, axis):
    count = len(blocks)
    here = lax.axis_index(axis)
    mine = blocks[count - 1]
    for index in range(count - 1):
        got = lax.ppermute(blocks[index], axis, [(count - 1, index)])
        mine = jnp.where(here == index, got, mine)
    return mine


def body(states, w_query, w_key, w_value):
    local = states[0]
    rows = local.shape[0]
    steps = lax.axis_size("depth")
    part = rows // steps
    shards = lax.axis_size("tok")
    queries = project_q(local, w_query, steps)
    kv = project_kv(local, w_key, w_value)
    rim = lax.ppermute(kv[rows - WINDOW :], "tok", [(t, t + 1) for t in range(shards - 1)])
    spread = lax.all_to_all(kv.reshape(steps, part, kv.shape[1]), "depth", split_axis=0, concat_axis=0, tiled=True)
    first = (lax.axis_index("tok") == 0).astype(jnp.int32).reshape(1)
    window_out = band_attend(queries, kv, rim, first)
    final_q = scatter_last(queries, "depth")
    depth_out = depth_attend(final_q, spread)
    return (window_out[None], depth_out)


def solution(mesh):
    in_specs = (P("depth", "tok", None), P(), P(), P())
    out_specs = (P("depth", "tok", None), P(("tok", "depth"), None))
    return jax.shard_map(body, mesh=mesh, in_specs=in_specs, out_specs=out_specs, check_vma=False)
```

time: 146 us -> 75.5 us (0.52)
  the two profiles are of different devices: /device:TPU:16 before, /device:TPU:0 now
where the time goes in v1:
time: 75.5 us; the launch traced here: 74.9 us
  waiting for transfers between devices  27.9 us (37%)
  Pallas kernels  24 us (32%)
  starting transfers between devices  17.1 us (23%)
  local copies, waits for them, and re-layouts  4.17 us (6%)
  other arithmetic  1.07 us (1%)
    ppermute x7, waiting for transfers between devices, scatter_last(): got = lax.ppermute(blocks[index], axis, [(count - 1, index)])  27.9 us
    ppermute x7, starting transfers between devices, scatter_last(): got = lax.ppermute(blocks[index], axis, [(count - 1, index)])  8.34 us
    pallas_call x1, Pallas kernels, band_attend(): pl.pallas_call(functools.partial(band_kernel, parts), out_shape=jax.Shape...  8.29 us
    pallas_call x1, Pallas kernels, project_q(): pl.pallas_call(project_q_kernel, out_shape=[jax.ShapeDtypeStruct((part, w...  7.98 us
    all_to_all x1, starting transfers between devices, body(): lax.all_to_all(kv.reshape(steps, part, kv.shape[1]), 'depth', split_axis=...  7.25 us
    pallas_call x1, Pallas kernels, project_kv(): pl.pallas_call(project_kv_kernel, grid=(count // block,), out_shape=jax.S...  5.48 us
    unnamed x12, local copies, waits for them, and re-layouts  3.17 us
    pallas_call x1, Pallas kernels, depth_attend(): pl.pallas_call(depth_kernel, out_shape=jax.ShapeDtypeStruct(query.shape,...  2.28 us
  transfers between devices with their start and end apart: 9, of which 1 were waited for; matrix products, arithmetic and copies ran while one was open for 3% of the time, Pallas kernels for 22%

profile of v1, /device:TPU:0, one launch (start us, length us, event | category | flops | bytes accessed | tf_op | source)
XLA Modules:
  0.0 74.9 jit_solution(965338544327156991)
XLA Ops:
  0.6 1.2 %copy-done = bf16[2048,256]{1,0:T(8,128)(2,1)S(1)} copy-done((bf16[2048,256]{1,0:T(8,128)(2,1)S(1)}, bf16[2048,256]{1,0:T(8,128)(2,1)}, u32[]{:S(2)}) %copy-start) | copy-done | bytes 1048600
  1.9 1.2 %copy-done.1 = bf16[2048,256]{1,0:T(8,128)(2,1)S(1)} copy-done((bf16[2048,256]{1,0:T(8,128)(2,1)S(1)}, bf16[2048,256]{1,0:T(8,128)(2,1)}, u32[]{:S(2)}) %copy-start.1) | copy-done | bytes 1048600
  3.1 5.5 %shard_map.60.refs_8_ = bf16[1024,512]{1,0:T(8,128)(2,1)} custom-call(bf16[1024,2048]{1,0:T(8,128)(2,1)} %bitcast.4, bf16[2048,256]{1,0:T(8,128)(2,1)S(1)} %copy-done, bf16[2048,256]{1,0:T(8,128)(2,1)S(1)} %copy-done.1), custom_call_target="tpu_custom_call" | custom-call | flops 2147483648 | bytes 7340032 | tf_op jit(solution)/shard_map/pallas_call | solution.py:66
  8.6 7.3 %all-to-all-start = ((bf16[8,128,512]{2,1,0:T(8,128)(2,1)}), bf16[8,128,512]{2,1,0:T(8,128)(2,1)S(1)}, u32[]{:S(2)}, u32[]{:S(2)}) async-start(bf16[8,128,512]{2,1,0:T(8,128)(2,1)} %bitcast.3), calls=%async_computation | async-start | bytes 2097152 | tf_op jit(solution)/shard_map/all_to_all | solution.py:221
  15.8 1.0 %slice.4 = bf16[256,512]{1,0:T(8,128)(2,1)S(1)} slice(bf16[1024,512]{1,0:T(8,128)(2,1)} %shard_map.60.refs_8_), slice={[768:1024], [0:512]} | slice | bytes 524288 | tf_op jit(solution)/shard_map/slice | solution.py:220
  16.8 1.5 %collective-permute-start = (bf16[256,512]{1,0:T(8,128)(2,1)S(1)}, bf16[256,512]{1,0:T(8,128)(2,1)S(1)}, u32[]{:S(2)}, u32[]{:S(2)}) collective-permute-start(bf16[256,512]{1,0:T(8,128)(2,1)S(1)} %slice.4), channel_id=1, source_target_pairs={{0,1},{1,2},{2,3},{4,5},{5,6},{6,7},{8,9},{9,10},{10,11},{12,13},{... | collective-permute-start | bytes 786440 | tf_op jit(solution)/shard_map/ppermute | solution.py:220
  18.3 8.0 %shard_map.59 = (bf16[128,1024]{1,0:T(8,128)(2,1)S(1)}, bf16[128,1024]{1,0:T(8,128)(2,1)S(1)}, bf16[128,1024]{1,0:T(8,128)(2,1)S(1)}, bf16[128,1024]{1,0:T(8,128...) custom-call(bf16[1024,2048]{1,0:T(8,128)(2,1)} %bitcast.5, ...), custom_call_target="tpu_custom_call" | custom-call | flops 4294967296 | bytes 10485760 | tf_op jit(solution)/shard_map/pallas_call | solution.py:40
  26.3 0.7 collective-permute-start.1
  27.0 0.7 collective-permute-start.2
  27.7 1.4 %collective-permute-start.3 = (bf16[128,1024]{1,0:T(8,128)(2,1)S(1)}, bf16[128,1024]{1,0:T(8,128)(2,1)}, u32[]{:S(2)}, u32[]{:S(2)}) collective-permute-start(bf16[128,1024]{1,0:T(8,128)(2,1)S(1)} %get-tuple-element.14.refs_4_), channel_id=1, source_target_pairs={{28,16},{29,17},{30,18},{31,19}} | collective-permute-start | bytes 786440 | tf_op jit(solution)/shard_map/ppermute | solution.py:207
  29.1 1.4 %collective-permute-start.4 = (bf16[128,1024]{1,0:T(8,128)(2,1)S(1)}, bf16[128,1024]{1,0:T(8,128)(2,1)}, u32[]{:S(2)}, u32[]{:S(2)}) collective-permute-start(bf16[128,1024]{1,0:T(8,128)(2,1)S(1)} %get-tuple-element.13.refs_3_), channel_id=1, source_target_pairs={{28,12},{29,13},{30,14},{31,15}} | collective-permute-start | bytes 786440 | tf_op jit(solution)/shard_map/ppermute | solution.py:207
  30.4 0.0 collective-permute-done.refs_9_
  30.4 1.4 %collective-permute-start.5 = (bf16[128,1024]{1,0:T(8,128)(2,1)S(1)}, bf16[128,1024]{1,0:T(8,128)(2,1)}, u32[]{:S(2)}, u32[]{:S(2)}) collective-permute-start(bf16[128,1024]{1,0:T(8,128)(2,1)S(1)} %get-tuple-element.12.refs_2_), channel_id=1, source_target_pairs={{28,8},{29,9},{30,10},{31,11}} | collective-permute-start | bytes 786440 | tf_op jit(solution)/shard_map/ppermute | solution.py:207
  31.8 0.0 collective-permute-done.1
  31.8 1.4 %collective-permute-start.6 = (bf16[128,1024]{1,0:T(8,128)(2,1)S(1)}, bf16[128,1024]{1,0:T(8,128)(2,1)}, u32[]{:S(2)}, u32[]{:S(2)}) collective-permute-start(bf16[128,1024]{1,0:T(8,128)(2,1)S(1)} %get-tuple-element.11.refs_1_), channel_id=1, source_target_pairs={{28,4},{29,5},{30,6},{31,7}} | collective-permute-start | bytes 786440 | tf_op jit(solution)/shard_map/ppermute | solution.py:207
  33.2 0.7 copy-done.4
  33.9 1.5 %collective-permute-start.7 = (bf16[128,1024]{1,0:T(8,128)(2,1)S(1)}, bf16[128,1024]{1,0:T(8,128)(2,1)}, u32[]{:S(2)}, u32[]{:S(2)}) collective-permute-start(bf16[128,1024]{1,0:T(8,128)(2,1)S(1)} %get-tuple-element.10.refs_0_), channel_id=1, source_target_pairs={{28,0},{29,1},{30,2},{31,3}} | collective-permute-start | bytes 786440 | tf_op jit(solution)/shard_map/ppermute | solution.py:207
  35.4 0.0 copy-start.3
  35.4 8.3 %shard_map.61 = bf16[1024,1024]{1,0:T(8,128)(2,1)} custom-call(s32[1]{0:T(128)} %bitcast.first_ref, bf16[128,1024]{1,0:T(8,128)(2,1)S(1)} %get-tuple-element.10.refs_0_, bf16[128,1024]{1,0:T(8,128)(2,1)S(1)} %get-tuple-element.11.refs_1_, bf16[128,1024]{1,0:T(8,128)(2,1)S(1)} %get-tuple-element.12.refs_2_, bf16[128,1024]{1,0:T(8,128)(2,1)S(1)} %get-tuple-element.13.refs_3_, ...), custom_call_target="tpu_custom_call" | custom-call | flops 1610612736 | bytes 5242880 | tf_op jit(solution)/shard_map/pallas_call | solution.py:151
  43.7 0.0 collective-permute-done.3
  43.7 0.0 collective-permute-done.4
  43.7 27.8 %collective-permute-done.7 = bf16[128,1024]{1,0:T(8,128)(2,1)} collective-permute-done((bf16[128,1024]{1,0:T(8,128)(2,1)S(1)}, bf16[128,1024]{1,0:T(8,128)(2,1)}, u32[]{:S(2)}, u32[]{:S(2)}) %collective-permute-start.7) | collective-permute-done | bytes 262176 | tf_op jit(solution)/shard_map/ppermute | solution.py:207
  71.6 1.1 %select_select_fusion.q_ref = bf16[128,1024]{1,0:T(8,128)(2,1)S(1)} fusion(bf16[128,1024]{1,0:T(8,128)(2,1)S(1)} %copy-done.3, bf16[128,1024]{1,0:T(8,128)(2,1)S(1)} %copy-done.5, bf16[128,1024]{1,0:T(8,128)(2,1)} %collective-permute-done.3, bf16[128,1024]{1,0:T(8,128)(2,1)} %collective-permute-done.4, bf16[128,1024]{1,0:T(8,128)(2,1)} %collective-permute-done.5, ...), kind=kLoop, calls=%fused_computation | loop fusion | flops 917504 | bytes 2359303 | tf_op jit(solution)/shard_map/jit(_where)/select_n | solution.py:208
  72.7 2.3 %shard_map.62 = bf16[128,1024]{1,0:T(8,128)(2,1)} custom-call(bf16[128,1024]{1,0:T(8,128)(2,1)S(1)} %select_select_fusion.q_ref, bf16[8,128,512]{2,1,0:T(8,128)(2,1)S(1)} %all-to-all-done.kv_ref), custom_call_target="tpu_custom_call" | custom-call | flops 4194304 | bytes 1572864 | tf_op jit(solution)/shard_map/pallas_call | solution.py:188
  (12 shorter events, 0.0 us)
Async XLA Ops:
  0.6 1.2 %copy-start = (bf16[2048,256]{1,0:T(8,128)(2,1)S(1)}, bf16[2048,256]{1,0:T(8,128)(2,1)}, u32[]{:S(2)}) copy-start(bf16[2048,256]{1,0:T(8,128)(2,1)} %wk_ref.1) | copy-start | bytes 3145732
  1.9 1.2 %copy-start.1 = (bf16[2048,256]{1,0:T(8,128)(2,1)S(1)}, bf16[2048,256]{1,0:T(8,128)(2,1)}, u32[]{:S(2)}) copy-start(bf16[2048,256]{1,0:T(8,128)(2,1)} %wv_ref.1) | copy-start | bytes 3145732
  8.6 64.1 %all-to-all-start = ((bf16[8,128,512]{2,1,0:T(8,128)(2,1)}), bf16[8,128,512]{2,1,0:T(8,128)(2,1)S(1)}, u32[]{:S(2)}, u32[]{:S(2)}) async-start(bf16[8,128,512]{2,1,0:T(8,128)(2,1)} %bitcast.3), calls=%async_computation | async-start | bytes 2097152 | tf_op jit(solution)/shard_map/all_to_all | solution.py:221
  16.8 13.6 %collective-permute-start = (bf16[256,512]{1,0:T(8,128)(2,1)S(1)}, bf16[256,512]{1,0:T(8,128)(2,1)S(1)}, u32[]{:S(2)}, u32[]{:S(2)}) collective-permute-start(bf16[256,512]{1,0:T(8,128)(2,1)S(1)} %slice.4), channel_id=1, source_target_pairs={{0,1},{1,2},{2,3},{4,5},{5,6},{6,7},{8,9},{9,10},{10,11},{12,13},{... | collective-permute-start | bytes 786440 | tf_op jit(solution)/shard_map/ppermute | solution.py:220
  26.3 5.5 %collective-permute-start.1 = (bf16[128,1024]{1,0:T(8,128)(2,1)S(1)}, bf16[128,1024]{1,0:T(8,128)(2,1)S(1)}, u32[]{:S(2)}, u32[]{:S(2)}) collective-permute-start(bf16[128,1024]{1,0:T(8,128)(2,1)S(1)} %get-tuple-element.16.refs_6_), channel_id=1, source_target_pairs={{28,24},{29,25},{30,26},{31,27}} | collective-permute-start | bytes 786440 | tf_op jit(solution)/shard_map/ppermute | solution.py:207
  27.0 6.2 %collective-permute-start.2 = (bf16[128,1024]{1,0:T(8,128)(2,1)S(1)}, bf16[128,1024]{1,0:T(8,128)(2,1)S(1)}, u32[]{:S(2)}, u32[]{:S(2)}) collective-permute-start(bf16[128,1024]{1,0:T(8,128)(2,1)S(1)} %get-tuple-element.15.refs_5_), channel_id=1, source_target_pairs={{28,20},{29,21},{30,22},{31,23}} | collective-permute-start | bytes 786440 | tf_op jit(solution)/shard_map/ppermute | solution.py:207
  27.7 16.1 %collective-permute-start.3 = (bf16[128,1024]{1,0:T(8,128)(2,1)S(1)}, bf16[128,1024]{1,0:T(8,128)(2,1)}, u32[]{:S(2)}, u32[]{:S(2)}) collective-permute-start(bf16[128,1024]{1,0:T(8,128)(2,1)S(1)} %get-tuple-element.14.refs_4_), channel_id=1, source_target_pairs={{28,16},{29,17},{30,18},{31,19}} | collective-permute-start | bytes 786440 | tf_op jit(solution)/shard_map/ppermute | solution.py:207
  29.1 14.7 %collective-permute-start.4 = (bf16[128,1024]{1,0:T(8,128)(2,1)S(1)}, bf16[128,1024]{1,0:T(8,128)(2,1)}, u32[]{:S(2)}, u32[]{:S(2)}) collective-permute-start(bf16[128,1024]{1,0:T(8,128)(2,1)S(1)} %get-tuple-element.13.refs_3_), channel_id=1, source_target_pairs={{28,12},{29,13},{30,14},{31,15}} | collective-permute-start | bytes 786440 | tf_op jit(solution)/shard_map/ppermute | solution.py:207
  30.4 13.3 %collective-permute-start.5 = (bf16[128,1024]{1,0:T(8,128)(2,1)S(1)}, bf16[128,1024]{1,0:T(8,128)(2,1)}, u32[]{:S(2)}, u32[]{:S(2)}) collective-permute-start(bf16[128,1024]{1,0:T(8,128)(2,1)S(1)} %get-tuple-element.12.refs_2_), channel_id=1, source_target_pairs={{28,8},{29,9},{30,10},{31,11}} | collective-permute-start | bytes 786440 | tf_op jit(solution)/shard_map/ppermute | solution.py:207
  31.8 1.4 %copy-start.2 = (bf16[128,1024]{1,0:T(8,128)(2,1)}, bf16[128,1024]{1,0:T(8,128)(2,1)S(1)}, u32[]{:S(2)}) copy-start(bf16[128,1024]{1,0:T(8,128)(2,1)S(1)} %collective-permute-done.1) | copy-start | bytes 786436
  31.8 11.9 %collective-permute-start.6 = (bf16[128,1024]{1,0:T(8,128)(2,1)S(1)}, bf16[128,1024]{1,0:T(8,128)(2,1)}, u32[]{:S(2)}, u32[]{:S(2)}) collective-permute-start(bf16[128,1024]{1,0:T(8,128)(2,1)S(1)} %get-tuple-element.11.refs_1_), channel_id=1, source_target_pairs={{28,4},{29,5},{30,6},{31,7}} | collective-permute-start | bytes 786440 | tf_op jit(solution)/shard_map/ppermute | solution.py:207
  33.2 0.7 copy-start.4
  33.9 37.7 %collective-permute-start.7 = (bf16[128,1024]{1,0:T(8,128)(2,1)S(1)}, bf16[128,1024]{1,0:T(8,128)(2,1)}, u32[]{:S(2)}, u32[]{:S(2)}) collective-permute-start(bf16[128,1024]{1,0:T(8,128)(2,1)S(1)} %get-tuple-element.10.refs_0_), channel_id=1, source_target_pairs={{28,0},{29,1},{30,2},{31,3}} | collective-permute-start | bytes 786440 | tf_op jit(solution)/shard_map/ppermute | solution.py:207
  35.4 36.2 %copy-start.3 = (bf16[128,1024]{1,0:T(8,128)(2,1)S(1)}, bf16[128,1024]{1,0:T(8,128)(2,1)}, u32[]{:S(2)}) copy-start(bf16[128,1024]{1,0:T(8,128)(2,1)} %copy-done.2) | copy-start | bytes 786436
  35.4 36.2 %copy-start.5 = (bf16[128,1024]{1,0:T(8,128)(2,1)S(1)}, bf16[128,1024]{1,0:T(8,128)(2,1)}, u32[]{:S(2)}) copy-start(bf16[128,1024]{1,0:T(8,128)(2,1)} %copy-done.4) | copy-start | bytes 786436

commit v2 on v1

v2 whole, which is shorter than its diff:
```python
import functools
import math

import jax
import jax.numpy as jnp
from jax import lax
from jax.experimental import pallas as pl
from jax.experimental.pallas import tpu as pltpu
from jax.sharding import PartitionSpec as P

HQ = 8
HK = 2
HD = 128
WINDOW = 256
GROUP = HQ // HK
SCALE = 1.0 / math.sqrt(HD)
BAND = 128
RELAYS = 2
LAST_FLOPS = 10**9
MIB = 1024 * 1024
VMEM = pl.BlockSpec(memory_space=pltpu.VMEM)
SMEM = pl.BlockSpec(memory_space=pltpu.SMEM)
ANY = pl.BlockSpec(memory_space=pl.ANY)
HBM = pl.BlockSpec(memory_space=pltpu.HBM)


def params(mib):
    return pltpu.CompilerParams(vmem_limit_bytes=mib * MIB)


def array(*shape):
    return jax.ShapeDtypeStruct(shape, jnp.bfloat16)


def buffer(*shape):
    return pltpu.VMEM(shape, jnp.bfloat16)


def hbm_array(*shape):
    return pltpu.HBM(shape, jnp.bfloat16)


def in_hbm(*arrays):
    return [pltpu.with_memory_space_constraint(a, pltpu.HBM) for a in arrays]


def cost(flops=1):
    return pl.CostEstimate(flops=flops, bytes_accessed=1, transcendentals=0)


def matmul(x, w):
    return jnp.dot(x, w, preferred_element_type=jnp.float32).astype(jnp.bfloat16)


def project_kv_kernel(x_hbm, wk_hbm, wv_hbm, kv_hbm, rim_hbm, kv_ref, x_ref, wk_ref, wv_ref, in_sems, out_sems):
    chunks, size = x_ref.shape[:2]
    width = wk_ref.shape[1]
    slices = [pl.ds(i * size, size) for i in range(chunks)]
    load_k = pltpu.make_async_copy(wk_hbm, wk_ref, in_sems.at[0])
    load_v = pltpu.make_async_copy(wv_hbm, wv_ref, in_sems.at[1])
    load_x = [
        pltpu.make_async_copy(x_hbm.at[at], x_ref.at[i], in_sems.at[2 + i]) for i, at in enumerate(slices)
    ]
    load_k.start()
    load_x[0].start()
    load_v.start()
    for load in load_x[1:]:
        load.start()
    load_k.wait()
    stores = []
    for i, at in enumerate(slices):
        load_x[i].wait()
        kv_ref[at, :width] = matmul(x_ref[i], wk_ref[...])
        if not i:
            load_v.wait()
        kv_ref[at, width:] = matmul(x_ref[i], wv_ref[...])
        stores.append(pltpu.make_async_copy(kv_ref.at[at], kv_hbm.at[at], out_sems.at[i]))
        stores[-1].start()
    last = pl.ds(chunks * size - WINDOW, WINDOW)
    stores.append(pltpu.make_async_copy(kv_ref.at[last], rim_hbm, out_sems.at[chunks]))
    stores[-1].start()
    for store in stores:
        store.wait()


def project_kv(rows, w_key, w_value):
    count, depth = rows.shape
    width = w_key.shape[1]
    size = min(count, 256)
    chunks = count // size
    return pl.pallas_call(
        project_kv_kernel,
        out_shape=[hbm_array(count, 2 * width), hbm_array(WINDOW, 2 * width), array(count, 2 * width)],
        in_specs=[HBM] * 3,
        out_specs=[HBM] * 2 + [VMEM],
        scratch_shapes=[
            buffer(chunks, size, depth),
            buffer(depth, width),
            buffer(depth, width),
            pltpu.SemaphoreType.DMA((2 + chunks,)),
            pltpu.SemaphoreType.DMA((1 + chunks,)),
        ],
        compiler_params=params(16),
        cost_estimate=cost(),
    )(*in_hbm(rows, w_key, w_value))


def project_q_kernel(part, pick, x_hbm, w_hbm, q_ref, *refs):
    out_refs, (x_ref, w_ref, in_sems, out_sems) = refs[:-4], refs[-4:]
    chunks, size = x_ref.shape[:2]
    slices = [pl.ds(i * size, size) for i in range(chunks)]
    load_w = pltpu.make_async_copy(w_hbm, w_ref, in_sems.at[chunks])
    load_x = [pltpu.make_async_copy(x_hbm.at[at], x_ref.at[i], in_sems.at[i]) for i, at in enumerate(slices)]
    load_w.start()
    for load in load_x:
        load.start()
    load_w.wait()
    stores = []
    for i, at in enumerate(slices):
        load_x[i].wait()
        q_ref[at, :] = matmul(x_ref[i], w_ref[...])
        for number, index in enumerate(pick):
            if i * size < (index + 1) * part <= (i + 1) * size:
                source = q_ref.at[pl.ds(index * part, part)]
                stores.append(pltpu.make_async_copy(source, out_refs[number], out_sems.at[number]))
                stores[-1].start()
    for store in stores:
        store.wait()


def project_q(rows, weight, part, pick):
    count = rows.shape[0]
    depth, width = weight.shape
    size = min(count, 256)
    return pl.pallas_call(
        functools.partial(project_q_kernel, part, pick),
        out_shape=[array(count, width)] + [hbm_array(part, width)] * len(pick),
        in_specs=[HBM] * 2,
        out_specs=[VMEM] + [HBM] * len(pick),
        scratch_shapes=[
            buffer(count // size, size, depth),
            buffer(depth, width),
            pltpu.SemaphoreType.DMA((1 + count // size,)),
            pltpu.SemaphoreType.DMA((len(pick),)),
        ],
        compiler_params=params(16),
        cost_estimate=cost(),
    )(*in_hbm(rows, weight))


def choose_kernel(which_ref, a_hbm, b_hbm, *refs):
    out_ref, sem = refs[-2:]
    for flag, source in ((1, a_hbm), (0, b_hbm)):

        @pl.when(which_ref[0] == flag)
        def _(source=source):
            pltpu.make_async_copy(source, out_ref, sem).start()

    pltpu.make_async_copy(b_hbm, out_ref, sem).wait()


def choose(which, a, b, after):
    return pl.pallas_call(
        choose_kernel,
        out_shape=array(*a.shape),
        in_specs=[SMEM] + [HBM] * 2 + [ANY] * len(after),
        out_specs=VMEM,
        scratch_shapes=[pltpu.SemaphoreType.DMA],
        compiler_params=params(16),
        cost_estimate=cost(),
    )(which, *in_hbm(a, b), *after)


def band_kernel(blocks_of, first_ref, q_ref, kv_ref, *refs):
    rim_ref, (out_hbm, token_ref, out_ref, sems) = refs[0], refs[-4:]
    token_ref[...] = jnp.zeros_like(token_ref)
    width = kv_ref.shape[1] // 2
    first = first_ref[0] == 1
    row = lax.broadcasted_iota(jnp.int32, (GROUP * BAND, BAND), 0) % BAND
    column = lax.broadcasted_iota(jnp.int32, (GROUP * BAND, BAND), 1)
    behind = column >= row
    ahead = column <= row
    ones = jnp.ones((BAND, HD), jnp.bfloat16)

    def chunk(index, low, high):
        if index < 0:
            return rim_ref[pl.ds(WINDOW + index * BAND, BAND), low:high]
        return kv_ref[pl.ds(index * BAND, BAND), low:high]

    blocks = WINDOW // BAND + 1
    stores = []
    for number, index in enumerate(blocks_of):
        for c in range(HK):
            q = jnp.concatenate(
                [q_ref[pl.ds(index * BAND, BAND), h * HD : (h + 1) * HD] for h in range(c * GROUP, (c + 1) * GROUP)],
                axis=0,
            )
            at = [index + j - (blocks - 1) for j in range(blocks)]
            k = jnp.concatenate([chunk(a, c * HD, (c + 1) * HD) for a in at], axis=0)
            v = jnp.concatenate([chunk(a, width + c * HD, width + (c + 1) * HD) for a in at], axis=0)
            v = jnp.concatenate([v, jnp.concatenate([ones] * blocks, axis=0)], axis=1)
            s = lax.dot_general(q, k, (((1,), (1,)), ((), ())), preferred_element_type=jnp.float32)
            tiles = []
            for j in range(blocks):
                t = s[:, j * BAND : (j + 1) * BAND]
                allowed = None
                if j == 0:
                    allowed = behind
                elif j == blocks - 1:
                    allowed = ahead
                if at[j] < 0:
                    some = jnp.logical_not(first)
                    allowed = some if allowed is None else jnp.logical_and(allowed, some)
                if allowed is not None:
                    t = jnp.where(allowed, t, -jnp.inf)
                tiles.append(t)
            top = functools.reduce(jnp.maximum, tiles)
            top = jnp.max(top, axis=-1, keepdims=True)
            p = jnp.concatenate(
                [jnp.exp2((t - top) * (SCALE * math.log2(math.e))).astype(jnp.bfloat16) for t in tiles], axis=1
            )
            o = jnp.dot(p, v, preferred_element_type=jnp.float32)
            o = (o[:, :HD] / o[:, HD:]).astype(jnp.bfloat16)
            for g in range(GROUP):
                h = c * GROUP + g
                out_ref[pl.ds(number * BAND, BAND), h * HD : (h + 1) * HD] = o[g * BAND : (g + 1) * BAND]
        stores.append(
            pltpu.make_async_copy(
                out_ref.at[pl.ds(number * BAND, BAND)], out_hbm.at[pl.ds(index * BAND, BAND)], sems.at[number]
            )
        )
        stores[-1].start()
    for store in stores:
        store.wait()


def band_attend(first, query, kv, rim, blocks_of, out, after, flops=1):
    count, width = query.shape
    rows = len(blocks_of) * BAND
    inside = [rim] if blocks_of[0] * BAND < WINDOW else []
    given = [] if out is None else [out]
    return pl.pallas_call(
        functools.partial(band_kernel, blocks_of),
        out_shape=[array(count, width), array(16, HD)],
        in_specs=[SMEM] + [VMEM] * (2 + len(inside)) + [ANY] * len(given + after),
        out_specs=[ANY, VMEM],
        scratch_shapes=[buffer(rows, width), pltpu.SemaphoreType.DMA((len(blocks_of),))],
        input_output_aliases={3 + len(inside): 0} if given else {},
        compiler_params=params(16),
        cost_estimate=cost(flops),
    )(first, query, kv, *inside, *given, *after)


def depth_kernel(which_ref, *refs):
    q_refs, (kv_ref, out_ref, q_ref) = refs[:-3], refs[-3:]
    steps, count, width = kv_ref.shape
    width //= 2
    for case, ref in enumerate(q_refs):

        @pl.when(which_ref[0] == case)
        def _(ref=ref):
            q_ref[...] = ref[...]

    chunk = min(count, 32)
    for start in range(0, count, chunk):
        rows = pl.ds(start, chunk)
        for c in range(HK):
            keys = [kv_ref[s, rows, c * HD : (c + 1) * HD].astype(jnp.float32) for s in range(steps)]
            values = [
                kv_ref[s, rows, width + c * HD : width + (c + 1) * HD].astype(jnp.float32) for s in range(steps)
            ]
            for h in range(c * GROUP, (c + 1) * GROUP):
                q = q_ref[rows, h * HD : (h + 1) * HD].astype(jnp.float32)
                scores = [jnp.sum(q * k, axis=-1, keepdims=True) * SCALE for k in keys]
                top = functools.reduce(jnp.maximum, scores)
                expo = [jnp.exp(s - top) for s in scores]
                total = functools.reduce(jnp.add, expo)
                out = functools.reduce(jnp.add, [e * v for e, v in zip(expo, values)])
                out_ref[rows, h * HD : (h + 1) * HD] = (out / total).astype(jnp.bfloat16)


def depth_attend(which, queries, kv):
    shape = queries[0].shape
    size = queries[0].size
    return pl.pallas_call(
        depth_kernel,
        out_shape=array(*shape),
        in_specs=[SMEM] + [VMEM] * (len(queries) + 1),
        out_specs=VMEM,
        scratch_shapes=[buffer(*shape)],
        compiler_params=params(16),
        cost_estimate=cost(),
    )(which, *queries, kv)


def flag(value):
    return value.astype(jnp.int32).reshape(1)


def body(states, w_query, w_key, w_value):
    local = states[0]
    rows = local.shape[0]
    steps = lax.axis_size("depth")
    here = lax.axis_index("depth")
    part = rows // steps
    shards = lax.axis_size("tok")
    root, buddy = steps - 1, steps - 2
    first = flag(lax.axis_index("tok") == 0)
    is_root = flag(here == root)
    by_buddy = list(range(0, buddy, 2))[:RELAYS]
    straight = [i for i in range(buddy) if i // 2 * 2 not in by_buddy]

    kv, rim, own = project_kv(local, w_key, w_value)
    spread = lax.all_to_all(kv.reshape(steps, part, kv.shape[1]), "depth", split_axis=0, concat_axis=0, tiled=True)
    rim = lax.ppermute(rim, "tok", [(t, t + 1) for t in range(shards - 1)])
    query, *queries = project_q(local, w_query, part, list(range(steps)))

    relayed = [lax.ppermute(queries[index], "depth", [(root, buddy)]) for index in by_buddy]
    direct = [lax.ppermute(queries[index], "depth", [(root, index)]) for index in straight]
    owners = [(queries[root], [root])] + [(q, [index]) for q, index in zip(direct, straight)]
    blocks = list(range(rows // BAND))
    calls = len(by_buddy) + 1
    window_out, after = None, []
    for turn in range(calls):
        low, high = len(blocks) * (calls - 1 - turn) // calls, len(blocks) * (calls - turn) // calls
        flops = LAST_FLOPS if turn == calls - 1 else 1
        window_out, token = band_attend(first, query, own, rim, blocks[low:high], window_out, after, flops)
        after = []
        if turn < calls - 1:
            index = by_buddy[turn]
            last = turn == calls - 2
            block = choose(is_root, queries[index + 1], relayed[turn], [token] + (direct if last else []))
            got = lax.ppermute(block, "depth", [(buddy, index), (root, index + 1)])
            owners.append((got, [index, index + 1]))
            if last:
                after = [q for q, _ in owners[1 + len(direct) : -1]]
    owners.append((lax.ppermute(queries[buddy], "depth", [(root, buddy)]), [buddy]))
    which = sum((jnp.where(here == i, case, 0) for case, (_, found) in enumerate(owners) for i in found), 0)
    depth_out = depth_attend(flag(which), [q for q, _ in owners], spread)
    return (window_out[None], depth_out)


def solution(mesh):
    in_specs = (P("depth", "tok", None), P(), P(), P())
    out_specs = (P("depth", "tok", None), P(("tok", "depth"), None))
    return jax.shard_map(body, mesh=mesh, in_specs=in_specs, out_specs=out_specs, check_vma=False)
```

time: 75.5 us -> 62.5 us (0.83)
  the two profiles are of different devices: /device:TPU:0 before, /device:TPU:11 now
where the time goes in v2:
time: 62.5 us; the launch traced here: 62.1 us
  Pallas kernels  31.4 us (50%)
  starting transfers between devices  19 us (30%)
  waiting for transfers between devices  9.99 us (16%)
  local copies, waits for them, and re-layouts  0.95 us (2%)
  between operations  0.8 us (1%)
    ppermute x2, waiting for transfers between devices, body(): got = lax.ppermute(block, 'depth', [(buddy, index), (root, index + 1)])  9.97 us
    pallas_call x3, Pallas kernels, band_attend(): pl.pallas_call(functools.partial(band_kernel, blocks_of), out_shape=[arra...  9.87 us
    pallas_call x1, Pallas kernels, project_q(): pl.pallas_call(functools.partial(project_q_kernel, part, pick), out_shape...  8.39 us
    pallas_call x1, Pallas kernels, project_kv(): pl.pallas_call(project_kv_kernel, out_shape=[hbm_array(count, 2 * width),...  5.94 us
    all_to_all x1, starting transfers between devices, body(): lax.all_to_all(kv.reshape(steps, part, kv.shape[1]), 'depth', split_axis=...  5.67 us
    ppermute x1, starting transfers between devices, body(): rim = lax.ppermute(rim, 'tok', [(t, t + 1) for t in range(shards - 1)])  4.26 us
    pallas_call x1, Pallas kernels, depth_attend(): pl.pallas_call(depth_kernel, out_shape=array(*shape), in_specs=[SMEM] + [...  3.85 us
    pallas_call x2, Pallas kernels, choose(): pl.pallas_call(choose_kernel, out_shape=array(*a.shape), in_specs=[SMEM]...  3.32 us
  transfers between devices with their start and end apart: 9, of which 1 were waited for; matrix products, arithmetic and copies ran while one was open for 0% of the time, Pallas kernels for 35%

profile of v2, /device:TPU:11, one launch (start us, length us, event | category | flops | bytes accessed | tf_op | source)
XLA Modules:
  0.0 62.1 jit_solution(16572002601129915867)
XLA Ops:
  0.6 5.9 %shard_map.60 = (bf16[1024,512]{1,0:T(8,128)(2,1)}, bf16[256,512]{1,0:T(8,128)(2,1)}, bf16[1024,512]{1,0:T(8,128)(2,1)S(1)}) custom-call(bf16[1024,2048]{1,0:T(8,128)(2,1)} %bitcast.6, bf16[2048,256]{1,0:T(8,128)(2,1)} %wk_hbm.1, bf16[2048,256]{1,0:T(8,128)(2,1)} %wv_hbm.1), custom_call_target="tpu_custom_call" | custom-call | flops 1 | bytes 1 | tf_op jit(solution)/shard_map/pallas_call | solution.py:91
  6.6 5.7 %all-to-all-start = ((bf16[8,128,512]{2,1,0:T(8,128)(2,1)}), bf16[8,128,512]{2,1,0:T(8,128)(2,1)}, u32[]{:S(2)}, u32[]{:S(2)}) async-start(bf16[8,128,512]{2,1,0:T(8,128)(2,1)} %bitcast.9), calls=%async_computation | async-start | bytes 2097152 | tf_op jit(solution)/shard_map/all_to_all | solution.py:314
  12.3 8.4 %shard_map.59 = (bf16[1024,1024]{1,0:T(8,128)(2,1)S(1)}, bf16[128,1024]{1,0:T(8,128)(2,1)}, bf16[128,1024]{1,0:T(8,128)(2,1)}, bf16[128,1024]{1,0:T(8,128)(2,1)}...) custom-call(bf16[1024,2048]{1,0:T(8,128)(2,1)} %bitcast.7, ...), custom_call_target="tpu_custom_call" | custom-call | flops 1 | bytes 1 | tf_op jit(solution)/shard_map/pallas_call | solution.py:135
  20.7 1.4 %collective-permute-start.1 = (bf16[128,1024]{1,0:T(8,128)(2,1)}, bf16[128,1024]{1,0:T(8,128)(2,1)}, u32[]{:S(2)}, u32[]{:S(2)}) collective-permute-start(bf16[128,1024]{1,0:T(8,128)(2,1)} %get-tuple-element.25), channel_id=1, source_target_pairs={{28,24},{29,25},{30,26},{31,27}} | collective-permute-start | bytes 786440 | tf_op jit(solution)/shard_map/ppermute | solution.py:318
  22.0 0.7 %collective-permute-start.3 = (bf16[128,1024]{1,0:T(8,128)(2,1)}, bf16[128,1024]{1,0:T(8,128)(2,1)S(1)}, u32[]{:S(2)}, u32[]{:S(2)}) collective-permute-start(bf16[128,1024]{1,0:T(8,128)(2,1)} %get-tuple-element.29), channel_id=1, source_target_pairs={{28,16},{29,17},{30,18},{31,19}} | collective-permute-start | bytes 786440 | tf_op jit(solution)/shard_map/ppermute | solution.py:319
  22.7 1.4 %collective-permute-start.4 = (bf16[128,1024]{1,0:T(8,128)(2,1)}, bf16[128,1024]{1,0:T(8,128)(2,1)}, u32[]{:S(2)}, u32[]{:S(2)}) collective-permute-start(bf16[128,1024]{1,0:T(8,128)(2,1)} %get-tuple-element.30), channel_id=1, source_target_pairs={{28,20},{29,21},{30,22},{31,23}} | collective-permute-start | bytes 786440 | tf_op jit(solution)/shard_map/ppermute | solution.py:319
  24.1 1.4 %collective-permute-start.5 = (bf16[128,1024]{1,0:T(8,128)(2,1)}, bf16[128,1024]{1,0:T(8,128)(2,1)}, u32[]{:S(2)}, u32[]{:S(2)}) collective-permute-start(bf16[128,1024]{1,0:T(8,128)(2,1)} %get-tuple-element.32), channel_id=1, source_target_pairs={{28,24},{29,25},{30,26},{31,27}} | collective-permute-start | bytes 786440 | tf_op jit(solution)/shard_map/ppermute | solution.py:318
  25.5 4.3 %collective-permute-start = (bf16[256,512]{1,0:T(8,128)(2,1)}, bf16[256,512]{1,0:T(8,128)(2,1)}, u32[]{:S(2)}, u32[]{:S(2)}) collective-permute-start(bf16[256,512]{1,0:T(8,128)(2,1)} %get-tuple-element.21), channel_id=1, source_target_pairs={{0,1},{1,2},{2,3},{4,5},{5,6},{6,7},{8,9},{9,10},{10,11},{12,13},{... | collective-permute-start | bytes 786440 | tf_op jit(solution)/shard_map/ppermute | solution.py:315
  29.7 3.0 %shard_map.61 = (bf16[1024,1024]{1,0:T(8,128)(2,1)}, bf16[16,128]{1,0:T(8,128)(2,1)S(1)}) custom-call(s32[1]{0:T(128)} %bitcast.first_ref, bf16[1024,1024]{1,0:T(8,128)(2,1)S(1)} %get-tuple-element.19.q_ref, bf16[1024,512]{1,0:T(8,128)(2,1)S(1)} %get-tuple-element.20.kv_ref), custom_call_target="tpu_custom_call" | custom-call | flops 1 | bytes 1 | tf_op jit(solution)/shard_map/pallas_call | solution.py:242
  32.7 0.0 collective-permute-done.1.b_hbm
  32.8 1.7 %shard_map.63 = bf16[128,1024]{1,0:T(8,128)(2,1)} custom-call(s32[1]{0:T(128)} %bitcast.2.which_ref, bf16[128,1024]{1,0:T(8,128)(2,1)} %get-tuple-element.24.a_hbm, bf16[128,1024]{1,0:T(8,128)(2,1)} %collective-permute-done.1.b_hbm, bf16[16,128]{1,0:T(8,128)(2,1)S(1)} %get-tuple-element.26.refs_0_), custom_call_target="tpu_custom_call" | custom-call | flops 1 | bytes 1 | tf_op jit(solution)/shard_map/pallas_call | solution.py:163
  34.4 1.4 %collective-permute-start.2 = (bf16[128,1024]{1,0:T(8,128)(2,1)}, bf16[128,1024]{1,0:T(8,128)(2,1)}, u32[]{:S(2)}, u32[]{:S(2)}) collective-permute-start(bf16[128,1024]{1,0:T(8,128)(2,1)} %shard_map.63), channel_id=1, source_target_pairs={{24,0},{28,4},{25,1},{29,5},{26,2},{30,6},{27,3},{31,7}} | collective-permute-start | bytes 786440 | tf_op jit(solution)/shard_map/ppermute | solution.py:333
  35.8 3.0 %shard_map.62 = (bf16[1024,1024]{1,0:T(8,128)(2,1)}, bf16[16,128]{1,0:T(8,128)(2,1)S(1)}) custom-call(s32[1]{0:T(128)} %bitcast.first_ref, bf16[1024,1024]{1,0:T(8,128)(2,1)S(1)} %get-tuple-element.19.q_ref, bf16[1024,512]{1,0:T(8,128)(2,1)S(1)} %get-tuple-element.20.kv_ref, ...), custom_call_target="tpu_custom_call", output_to_operand_aliasing={{0}: (3, {})} | custom-call | flops 1 | bytes 1 | tf_op jit(solution)/shard_map/pallas_call | solution.py:242
  38.8 0.0 collective-permute-done.3.refs_1_
  38.8 1.4 %collective-permute-start.7 = (bf16[128,1024]{1,0:T(8,128)(2,1)}, bf16[128,1024]{1,0:T(8,128)(2,1)}, u32[]{:S(2)}, u32[]{:S(2)}) collective-permute-start(bf16[128,1024]{1,0:T(8,128)(2,1)} %get-tuple-element.34), channel_id=1, source_target_pairs={{28,24},{29,25},{30,26},{31,27}} | collective-permute-start | bytes 786440 | tf_op jit(solution)/shard_map/ppermute | solution.py:337
  40.2 0.0 collective-permute-done.4.refs_2_
  40.2 1.7 %shard_map.65 = bf16[128,1024]{1,0:T(8,128)(2,1)} custom-call(s32[1]{0:T(128)} %bitcast.2.which_ref, bf16[128,1024]{1,0:T(8,128)(2,1)} %get-tuple-element.31.a_hbm, bf16[128,1024]{1,0:T(8,128)(2,1)} %collective-permute-done.5.b_hbm, bf16[16,128]{1,0:T(8,128)(2,1)S(1)} %get-tuple-element.33.refs_0_, bf16[128,1024]{1,0:T(8,128)(2,1)S(1)} %collective-permute-done.3.refs_1_, ...), custom_call_target="tpu_custom_call" | custom-call | flops 1 | bytes 1 | tf_op jit(solution)/shard_map/pallas_call | solution.py:163
  41.9 1.5 %collective-permute-start.6 = (bf16[128,1024]{1,0:T(8,128)(2,1)}, bf16[128,1024]{1,0:T(8,128)(2,1)}, u32[]{:S(2)}, u32[]{:S(2)}) collective-permute-start(bf16[128,1024]{1,0:T(8,128)(2,1)} %shard_map.65), channel_id=1, source_target_pairs={{24,8},{28,12},{25,9},{29,13},{26,10},{30,14},{27,11},{31,15}} | collective-permute-start | bytes 786440 | tf_op jit(solution)/shard_map/ppermute | solution.py:333
  43.4 0.0 collective-permute-done.2.refs_2_.refs_3_
  43.4 3.9 %shard_map.64 = (bf16[1024,1024]{1,0:T(8,128)(2,1)}, bf16[16,128]{1,0:T(8,128)(2,1)}) custom-call(s32[1]{0:T(128)} %bitcast.first_ref, bf16[1024,1024]{1,0:T(8,128)(2,1)S(1)} %get-tuple-element.19.q_ref, bf16[1024,512]{1,0:T(8,128)(2,1)S(1)} %get-tuple-element.20.kv_ref, ...), custom_call_target="tpu_custom_call", output_to_operand_aliasing={{0}: (4, {})} | custom-call | flops 1000000000 | bytes 1 | tf_op jit(solution)/shard_map/pallas_call | solution.py:242
  47.3 0.0 collective-permute-done.7.refs_5_
  47.3 10.0 %collective-permute-done.6.refs_4_ = bf16[128,1024]{1,0:T(8,128)(2,1)} collective-permute-done((bf16[128,1024]{1,0:T(8,128)(2,1)}, bf16[128,1024]{1,0:T(8,128)(2,1)}, u32[]{:S(2)}, u32[]{:S(2)}) %collective-permute-start.6) | collective-permute-done | bytes 262176 | tf_op jit(solution)/shard_map/ppermute | solution.py:333
  57.3 0.9 %copy-done = bf16[128,1024]{1,0:T(8,128)(2,1)S(1)} copy-done((bf16[128,1024]{1,0:T(8,128)(2,1)S(1)}, bf16[128,1024]{1,0:T(8,128)(2,1)}, u32[]{:S(2)}) %copy-start) | copy-done | bytes 262168
  58.2 3.9 %shard_map.66 = bf16[128,1024]{1,0:T(8,128)(2,1)} custom-call(s32[1]{0:T(128)} %bitcast.4.which_ref, bf16[128,1024]{1,0:T(8,128)(2,1)S(1)} %copy-done, bf16[128,1024]{1,0:T(8,128)(2,1)S(1)} %collective-permute-done.3.refs_1_, bf16[128,1024]{1,0:T(8,128)(2,1)} %collective-permute-done.4.refs_2_, bf16[128,1024]{1,0:T(8,128)(2,1)} %collective-permute-done.2.refs_2_.refs_3_, ...), custom_call_target="tpu_custom_call" | custom-call | flops 1 | bytes 1 | tf_op jit(solution)/shard_map/pallas_call | solution.py:285
  (4 shorter events, 0.0 us)
Async XLA Ops:
  6.6 50.7 %all-to-all-start = ((bf16[8,128,512]{2,1,0:T(8,128)(2,1)}), bf16[8,128,512]{2,1,0:T(8,128)(2,1)}, u32[]{:S(2)}, u32[]{:S(2)}) async-start(bf16[8,128,512]{2,1,0:T(8,128)(2,1)} %bitcast.9), calls=%async_computation | async-start | bytes 2097152 | tf_op jit(solution)/shard_map/all_to_all | solution.py:314
  20.7 12.1 %collective-permute-start.1 = (bf16[128,1024]{1,0:T(8,128)(2,1)}, bf16[128,1024]{1,0:T(8,128)(2,1)}, u32[]{:S(2)}, u32[]{:S(2)}) collective-permute-start(bf16[128,1024]{1,0:T(8,128)(2,1)} %get-tuple-element.25), channel_id=1, source_target_pairs={{28,24},{29,25},{30,26},{31,27}} | collective-permute-start | bytes 786440 | tf_op jit(solution)/shard_map/ppermute | solution.py:318
  22.0 16.8 %collective-permute-start.3 = (bf16[128,1024]{1,0:T(8,128)(2,1)}, bf16[128,1024]{1,0:T(8,128)(2,1)S(1)}, u32[]{:S(2)}, u32[]{:S(2)}) collective-permute-start(bf16[128,1024]{1,0:T(8,128)(2,1)} %get-tuple-element.29), channel_id=1, source_target_pairs={{28,16},{29,17},{30,18},{31,19}} | collective-permute-start | bytes 786440 | tf_op jit(solution)/shard_map/ppermute | solution.py:319
  22.7 17.5 %collective-permute-start.4 = (bf16[128,1024]{1,0:T(8,128)(2,1)}, bf16[128,1024]{1,0:T(8,128)(2,1)}, u32[]{:S(2)}, u32[]{:S(2)}) collective-permute-start(bf16[128,1024]{1,0:T(8,128)(2,1)} %get-tuple-element.30), channel_id=1, source_target_pairs={{28,20},{29,21},{30,22},{31,23}} | collective-permute-start | bytes 786440 | tf_op jit(solution)/shard_map/ppermute | solution.py:319
  24.1 16.1 %collective-permute-start.5 = (bf16[128,1024]{1,0:T(8,128)(2,1)}, bf16[128,1024]{1,0:T(8,128)(2,1)}, u32[]{:S(2)}, u32[]{:S(2)}) collective-permute-start(bf16[128,1024]{1,0:T(8,128)(2,1)} %get-tuple-element.32), channel_id=1, source_target_pairs={{28,24},{29,25},{30,26},{31,27}} | collective-permute-start | bytes 786440 | tf_op jit(solution)/shard_map/ppermute | solution.py:318
  25.5 17.9 %collective-permute-start = (bf16[256,512]{1,0:T(8,128)(2,1)}, bf16[256,512]{1,0:T(8,128)(2,1)}, u32[]{:S(2)}, u32[]{:S(2)}) collective-permute-start(bf16[256,512]{1,0:T(8,128)(2,1)} %get-tuple-element.21), channel_id=1, source_target_pairs={{0,1},{1,2},{2,3},{4,5},{5,6},{6,7},{8,9},{9,10},{10,11},{12,13},{... | collective-permute-start | bytes 786440 | tf_op jit(solution)/shard_map/ppermute | solution.py:315
  34.4 9.0 %collective-permute-start.2 = (bf16[128,1024]{1,0:T(8,128)(2,1)}, bf16[128,1024]{1,0:T(8,128)(2,1)}, u32[]{:S(2)}, u32[]{:S(2)}) collective-permute-start(bf16[128,1024]{1,0:T(8,128)(2,1)} %shard_map.63), channel_id=1, source_target_pairs={{24,0},{28,4},{25,1},{29,5},{26,2},{30,6},{27,3},{31,7}} | collective-permute-start | bytes 786440 | tf_op jit(solution)/shard_map/ppermute | solution.py:333
  38.8 8.5 %collective-permute-start.7 = (bf16[128,1024]{1,0:T(8,128)(2,1)}, bf16[128,1024]{1,0:T(8,128)(2,1)}, u32[]{:S(2)}, u32[]{:S(2)}) collective-permute-start(bf16[128,1024]{1,0:T(8,128)(2,1)} %get-tuple-element.34), channel_id=1, source_target_pairs={{28,24},{29,25},{30,26},{31,27}} | collective-permute-start | bytes 786440 | tf_op jit(solution)/shard_map/ppermute | solution.py:337
  41.9 15.4 %collective-permute-start.6 = (bf16[128,1024]{1,0:T(8,128)(2,1)}, bf16[128,1024]{1,0:T(8,128)(2,1)}, u32[]{:S(2)}, u32[]{:S(2)}) collective-permute-start(bf16[128,1024]{1,0:T(8,128)(2,1)} %shard_map.65), channel_id=1, source_target_pairs={{24,8},{28,12},{25,9},{29,13},{26,10},{30,14},{27,11},{31,15}} | collective-permute-start | bytes 786440 | tf_op jit(solution)/shard_map/ppermute | solution.py:333
  57.3 1.0 %copy-start = (bf16[128,1024]{1,0:T(8,128)(2,1)S(1)}, bf16[128,1024]{1,0:T(8,128)(2,1)}, u32[]{:S(2)}) copy-start(bf16[128,1024]{1,0:T(8,128)(2,1)} %get-tuple-element.28.refs_0_) | copy-start | bytes 786436

commit v3 on v2

v3 whole, which is shorter than its diff:
```python
import functools
import math

import jax
import jax.numpy as jnp
from jax import lax
from jax.experimental import pallas as pl
from jax.experimental.pallas import tpu as pltpu
from jax.sharding import PartitionSpec as P

HQ = 8
HK = 2
HD = 128
WINDOW = 256
GROUP = HQ // HK
SCALE = 1.0 / math.sqrt(HD)
BAND = 128
RELAYS = 2
LAST_FLOPS = 10**9
PIECES = 4
LAST_ROWS = 256
MIB = 1024 * 1024
VMEM = pl.BlockSpec(memory_space=pltpu.VMEM)
SMEM = pl.BlockSpec(memory_space=pltpu.SMEM)
ANY = pl.BlockSpec(memory_space=pl.ANY)
HBM = pl.BlockSpec(memory_space=pltpu.HBM)


def params(mib):
    return pltpu.CompilerParams(vmem_limit_bytes=mib * MIB)


def array(*shape):
    return jax.ShapeDtypeStruct(shape, jnp.bfloat16)


def buffer(*shape):
    return pltpu.VMEM(shape, jnp.bfloat16)


def hbm_array(*shape):
    return pltpu.HBM(shape, jnp.bfloat16)


def in_hbm(*arrays):
    return [pltpu.with_memory_space_constraint(a, pltpu.HBM) for a in arrays]


def cost(flops=1):
    return pl.CostEstimate(flops=flops, bytes_accessed=1, transcendentals=0)


def accumulate(loads, x_ref, w_ref, acc_ref, out_ref, store):
    pieces, count, _ = x_ref.shape
    for i in range(pieces):
        for load in loads[i]:
            load.wait()
        chunk = count if i < pieces - 1 else min(count, LAST_ROWS)
        for start in range(0, count, chunk):
            at = pl.ds(start, chunk)
            term = jnp.dot(x_ref[i, at, :], w_ref[i], preferred_element_type=jnp.float32)
            if i:
                term = acc_ref[at, :] + term
            if i < pieces - 1:
                acc_ref[at, :] = term
            else:
                out_ref[at, :] = term.astype(jnp.bfloat16)
                store(start, chunk)


def load_pieces(x_hbm, x_ref, w_hbms, w_ref, sems):
    pieces, _, size = x_ref.shape
    loads = []
    for i in range(pieces):
        at, left = pl.ds(i * size, size), 0
        loads.append([pltpu.make_async_copy(x_hbm.at[:, at], x_ref.at[i], sems.at[i, 0])])
        for number, w_hbm in enumerate(w_hbms):
            width = w_hbm.shape[1]
            target = w_ref.at[i, :, pl.ds(left, width)]
            loads[-1].append(pltpu.make_async_copy(w_hbm.at[at], target, sems.at[i, 1 + number]))
            left += width
        for load in loads[-1]:
            load.start()
    return loads


def project_kv_kernel(x_hbm, wk_hbm, wv_hbm, kv_hbm, rim_hbm, x_ref, w_ref, acc_ref, kv_ref, in_sems, out_sems):
    loads = load_pieces(x_hbm, x_ref, [wk_hbm, wv_hbm], w_ref, in_sems)
    stores = []

    def store(start, chunk):
        at = pl.ds(start, chunk)
        stores.append(pltpu.make_async_copy(kv_ref.at[at], kv_hbm.at[at], out_sems.at[len(stores)]))
        stores[-1].start()

    accumulate(loads, x_ref, w_ref, acc_ref, kv_ref, store)
    last = pl.ds(kv_ref.shape[0] - WINDOW, WINDOW)
    stores.append(pltpu.make_async_copy(kv_ref.at[last], rim_hbm, out_sems.at[len(stores)]))
    stores[-1].start()
    for copy in stores:
        copy.wait()


def project_kv(rows, w_key, w_value):
    count, depth = rows.shape
    width = w_key.shape[1]
    return pl.pallas_call(
        project_kv_kernel,
        out_shape=[hbm_array(count, 2 * width), hbm_array(WINDOW, 2 * width)],
        in_specs=[HBM] * 3,
        out_specs=[HBM] * 2,
        scratch_shapes=[
            buffer(PIECES, count, depth // PIECES),
            buffer(PIECES, depth // PIECES, 2 * width),
            pltpu.VMEM((count, 2 * width), jnp.float32),
            buffer(count, 2 * width),
            pltpu.SemaphoreType.DMA((PIECES, 3)),
            pltpu.SemaphoreType.DMA((1 + -(-count // min(count, LAST_ROWS)),)),
        ],
        compiler_params=params(16),
        cost_estimate=cost(),
    )(*in_hbm(rows, w_key, w_value))


def project_q_kernel(part, x_hbm, w_hbm, q_ref, *refs):
    part_hbms, (x_ref, w_ref, acc_ref, in_sems, out_sems) = refs[:-5], refs[-5:]
    loads = load_pieces(x_hbm, x_ref, [w_hbm], w_ref, in_sems)
    stores = []

    def store(start, chunk):
        for index in range(len(part_hbms)):
            if start < (index + 1) * part <= start + chunk:
                source = q_ref.at[pl.ds(index * part, part)]
                stores.append(pltpu.make_async_copy(source, part_hbms[index], out_sems.at[index]))
                stores[-1].start()

    accumulate(loads, x_ref, w_ref, acc_ref, q_ref, store)
    for copy in stores:
        copy.wait()


def project_q(rows, weight, parts):
    count, depth = rows.shape
    width = weight.shape[1]
    part = count // parts
    return pl.pallas_call(
        functools.partial(project_q_kernel, part),
        out_shape=[array(count, width)] + [hbm_array(part, width)] * (parts - 1),
        in_specs=[HBM] * 2,
        out_specs=[VMEM] + [HBM] * (parts - 1),
        scratch_shapes=[
            buffer(PIECES, count, depth // PIECES),
            buffer(PIECES, depth // PIECES, width),
            pltpu.VMEM((count, width), jnp.float32),
            pltpu.SemaphoreType.DMA((PIECES, 2)),
            pltpu.SemaphoreType.DMA((parts - 1,)),
        ],
        compiler_params=params(20),
        cost_estimate=cost(),
    )(*in_hbm(rows, weight))


def nothing_kernel(*refs):
    pass


def once(block, arrays):
    return pl.pallas_call(
        nothing_kernel,
        out_shape=hbm_array(*block.shape),
        in_specs=[HBM] + [ANY] * len(arrays),
        out_specs=HBM,
        input_output_aliases={0: 0},
        cost_estimate=cost(),
    )(*in_hbm(block), *arrays)


def choose_kernel(which_ref, a_hbm, b_hbm, *refs):
    out_ref, sem = refs[-2:]
    for flag, source in ((1, a_hbm), (0, b_hbm)):

        @pl.when(which_ref[0] == flag)
        def _(source=source):
            pltpu.make_async_copy(source, out_ref, sem).start()

    pltpu.make_async_copy(b_hbm, out_ref, sem).wait()


def choose(which, a, b, after):
    return pl.pallas_call(
        choose_kernel,
        out_shape=array(*a.shape),
        in_specs=[SMEM] + [HBM] * 2 + [ANY] * len(after),
        out_specs=VMEM,
        scratch_shapes=[pltpu.SemaphoreType.DMA],
        compiler_params=params(16),
        cost_estimate=cost(),
    )(which, *in_hbm(a, b), *after)


def band_kernel(blocks_of, first_ref, q_ref, kv_ref, *refs):
    rim_ref, (out_hbm, token_ref, out_ref, sems) = refs[0], refs[-4:]
    token_ref[...] = jnp.zeros_like(token_ref)
    width = kv_ref.shape[1] // 2
    first = first_ref[0] == 1
    row = lax.broadcasted_iota(jnp.int32, (GROUP * BAND, BAND), 0) % BAND
    column = lax.broadcasted_iota(jnp.int32, (GROUP * BAND, BAND), 1)
    behind = column >= row
    ahead = column <= row
    ones = jnp.ones((BAND, HD), jnp.bfloat16)

    def chunk(index, low, high):
        if index < 0:
            return rim_ref[pl.ds(WINDOW + index * BAND, BAND), low:high]
        return kv_ref[pl.ds(index * BAND, BAND), low:high]

    blocks = WINDOW // BAND + 1
    stores = []
    for number, index in enumerate(blocks_of):
        for c in range(HK):
            q = jnp.concatenate(
                [q_ref[pl.ds(index * BAND, BAND), h * HD : (h + 1) * HD] for h in range(c * GROUP, (c + 1) * GROUP)],
                axis=0,
            )
            at = [index + j - (blocks - 1) for j in range(blocks)]
            k = jnp.concatenate([chunk(a, c * HD, (c + 1) * HD) for a in at], axis=0)
            v = jnp.concatenate([chunk(a, width + c * HD, width + (c + 1) * HD) for a in at], axis=0)
            v = jnp.concatenate([v, jnp.concatenate([ones] * blocks, axis=0)], axis=1)
            s = lax.dot_general(q, k, (((1,), (1,)), ((), ())), preferred_element_type=jnp.float32)
            tiles = []
            for j in range(blocks):
                t = s[:, j * BAND : (j + 1) * BAND]
                allowed = None
                if j == 0:
                    allowed = behind
                elif j == blocks - 1:
                    allowed = ahead
                if at[j] < 0:
                    some = jnp.logical_not(first)
                    allowed = some if allowed is None else jnp.logical_and(allowed, some)
                if allowed is not None:
                    t = jnp.where(allowed, t, -jnp.inf)
                tiles.append(t)
            top = functools.reduce(jnp.maximum, tiles)
            top = jnp.max(top, axis=-1, keepdims=True)
            p = jnp.concatenate(
                [jnp.exp2((t - top) * (SCALE * math.log2(math.e))).astype(jnp.bfloat16) for t in tiles], axis=1
            )
            o = jnp.dot(p, v, preferred_element_type=jnp.float32)
            o = (o[:, :HD] / o[:, HD:]).astype(jnp.bfloat16)
            for g in range(GROUP):
                h = c * GROUP + g
                out_ref[pl.ds(number * BAND, BAND), h * HD : (h + 1) * HD] = o[g * BAND : (g + 1) * BAND]
        stores.append(
            pltpu.make_async_copy(
                out_ref.at[pl.ds(number * BAND, BAND)], out_hbm.at[pl.ds(index * BAND, BAND)], sems.at[number]
            )
        )
        stores[-1].start()
    for store in stores:
        store.wait()


def band_attend(first, query, kv, rim, blocks_of, out, after, flops=1):
    count, width = query.shape
    rows = len(blocks_of) * BAND
    inside = [rim] if blocks_of[0] * BAND < WINDOW else []
    given = [] if out is None else [out]
    return pl.pallas_call(
        functools.partial(band_kernel, blocks_of),
        out_shape=[array(count, width), array(16, HD)],
        in_specs=[SMEM] + [VMEM] * (2 + len(inside)) + [ANY] * len(given + after),
        out_specs=[ANY, VMEM],
        scratch_shapes=[buffer(rows, width), pltpu.SemaphoreType.DMA((len(blocks_of),))],
        input_output_aliases={3 + len(inside): 0} if given else {},
        compiler_params=params(16),
        cost_estimate=cost(flops),
    )(first, query, kv, *inside, *given, *after)


def depth_kernel(cases, which_ref, *refs):
    q_hbms, (kv_hbm, out_hbm, q_ref, kv_ref, out_ref, sems) = refs[:cases], refs[cases:]
    steps, count, width = kv_ref.shape
    width //= 2
    chunk = min(count, 32)
    chunks = [pl.ds(start, chunk) for start in range(0, count, chunk)]
    last = pl.ds(q_hbms[0].shape[0] - count, count)
    loads = []
    for case, source in enumerate([q_hbms[0].at[last], *q_hbms[1:]]):

        @pl.when(which_ref[0] == case)
        def _(source=source):
            pltpu.make_async_copy(source, q_ref, sems.at[0]).start()

    for i, rows in enumerate(chunks):
        loads.append(pltpu.make_async_copy(kv_hbm.at[:, rows], kv_ref.at[:, rows], sems.at[1 + i]))
        loads[-1].start()
    pltpu.make_async_copy(q_hbms[1], q_ref, sems.at[0]).wait()
    stores = []
    for i, rows in enumerate(chunks):
        loads[i].wait()
        for c in range(HK):
            keys = [kv_ref[s, rows, c * HD : (c + 1) * HD].astype(jnp.float32) for s in range(steps)]
            values = [
                kv_ref[s, rows, width + c * HD : width + (c + 1) * HD].astype(jnp.float32) for s in range(steps)
            ]
            for h in range(c * GROUP, (c + 1) * GROUP):
                q = q_ref[rows, h * HD : (h + 1) * HD].astype(jnp.float32) * (SCALE * math.log2(math.e))
                scores = [jnp.sum(q * k, axis=-1, keepdims=True) for k in keys]
                top = functools.reduce(jnp.maximum, scores)
                expo = [jnp.exp2(s - top) for s in scores]
                part = 1.0 / functools.reduce(jnp.add, expo)
                out = functools.reduce(jnp.add, [(e * part) * v for e, v in zip(expo, values)])
                out_ref[rows, h * HD : (h + 1) * HD] = out.astype(jnp.bfloat16)
        stores.append(pltpu.make_async_copy(out_ref.at[rows], out_hbm.at[rows], sems.at[1 + len(chunks) + i]))
        stores[-1].start()
    for store in stores:
        store.wait()


def depth_attend(which, query, queries, kv):
    steps, count, _ = kv.shape
    shape = (count, query.shape[1])
    return pl.pallas_call(
        functools.partial(depth_kernel, 1 + len(queries)),
        out_shape=array(*shape),
        in_specs=[SMEM, ANY] + [HBM] * len(queries) + [HBM],
        out_specs=ANY,
        scratch_shapes=[
            buffer(*shape),
            buffer(*kv.shape),
            buffer(*shape),
            pltpu.SemaphoreType.DMA((1 + 2 * -(-count // min(count, 32)),)),
        ],
        compiler_params=params(16),
        cost_estimate=cost(),
    )(which, query, *in_hbm(*queries, kv))


def flag(value):
    return value.astype(jnp.int32).reshape(1)


def body(states, w_query, w_key, w_value):
    local = states[0]
    rows = local.shape[0]
    steps = lax.axis_size("depth")
    here = lax.axis_index("depth")
    part = rows // steps
    shards = lax.axis_size("tok")
    root, buddy = steps - 1, steps - 2
    first = flag(lax.axis_index("tok") == 0)
    is_root = flag(here == root)
    by_buddy = list(range(0, buddy, 2))[-RELAYS:]
    straight = [i for i in range(buddy) if i // 2 * 2 not in by_buddy]

    def send(block, *pairs):
        return lax.ppermute(block, "depth", list(pairs))

    kv, rim = project_kv(local, w_key, w_value)
    spread = lax.all_to_all(kv.reshape(steps, part, kv.shape[1]), "depth", split_axis=0, concat_axis=0, tiled=True)
    rim = lax.ppermute(rim, "tok", [(t, (t + 1) % shards) for t in range(shards)])
    query, *queries = project_q(local, w_query, steps)

    relayed = [send(queries[index], (root, buddy)) for index in by_buddy]
    direct = [send(queries[index], (root, index)) for index in straight]
    blocks = list(range(rows // BAND))
    calls = len(by_buddy) + 1
    window_out, after, beside = None, [], []
    for turn in range(calls):
        low, high = len(blocks) * (calls - 1 - turn) // calls, len(blocks) * (calls - turn) // calls
        flops = LAST_FLOPS if turn == calls - 1 else 1
        window_out, token = band_attend(first, query, kv, rim, blocks[low:high], window_out, after, flops)
        if turn < calls - 1:
            index = by_buddy[turn]
            last = turn == calls - 2
            block = choose(is_root, queries[index + 1], relayed[turn], [token] + (direct if last else []))
            if last:
                after = list(beside)
            beside.append(send(block, (buddy, index), (root, index + 1)))
    own = send(once(queries[buddy], [block]), (root, buddy))
    owners = [[i] for i in straight] + [[i, i + 1] for i in by_buddy] + [[buddy]]
    which = sum((jnp.where(here == i, case + 1, 0) for case, ends in enumerate(owners) for i in ends), 0)
    depth_out = depth_attend(flag(which), query, direct + beside + [own], spread)
    return (window_out[None], depth_out)


def solution(mesh):
    in_specs = (P("depth", "tok", None), P(), P(), P())
    out_specs = (P("depth", "tok", None), P(("tok", "depth"), None))
    return jax.shard_map(body, mesh=mesh, in_specs=in_specs, out_specs=out_specs, check_vma=False)
```

time: 62.5 us -> 57.8 us (0.925)
  the two profiles are of different devices: /device:TPU:11 before, /device:TPU:2 now
where the time goes in v3:
time: 57.8 us; the launch traced here: 57.5 us
  Pallas kernels  29 us (50%)
  starting transfers between devices  15.2 us (26%)
  waiting for transfers between devices  12.5 us (22%)
  between operations  0.76 us (1%)
    ppermute x7, waiting for transfers between devices, send(): return lax.ppermute(block, 'depth', list(pairs))  11.9 us
    pallas_call x3, Pallas kernels, band_attend(): pl.pallas_call(functools.partial(band_kernel, blocks_of), out_shape=[arra...  9.85 us
    ppermute x7, starting transfers between devices, send(): return lax.ppermute(block, 'depth', list(pairs))  8.84 us
    pallas_call x1, Pallas kernels, project_q(): pl.pallas_call(functools.partial(project_q_kernel, part), out_shape=[arra...  7.47 us
    all_to_all x1, starting transfers between devices, body(): lax.all_to_all(kv.reshape(steps, part, kv.shape[1]), 'depth', split_axis=...  6.35 us
    pallas_call x1, Pallas kernels, project_kv(): pl.pallas_call(project_kv_kernel, out_shape=[hbm_array(count, 2 * width),...  4.78 us
    pallas_call x1, Pallas kernels, depth_attend(): pl.pallas_call(functools.partial(depth_kernel, 1 + len(queries)), out_sha...  3.59 us
    pallas_call x2, Pallas kernels, choose(): pl.pallas_call(choose_kernel, out_shape=array(*a.shape), in_specs=[SMEM]...  3.33 us
  transfers between devices with their start and end apart: 9, of which 2 were waited for; matrix products, arithmetic and copies ran while one was open for 0% of the time, Pallas kernels for 36%

profile of v3, /device:TPU:2, one launch (start us, length us, event | category | flops | bytes accessed | tf_op | source)
XLA Modules:
  0.0 57.5 jit_solution(9669147362864781007)
XLA Ops:
  0.6 4.8 %shard_map.60 = (bf16[1024,512]{1,0:T(8,128)(2,1)}, bf16[256,512]{1,0:T(8,128)(2,1)}) custom-call(bf16[1024,2048]{1,0:T(8,128)(2,1)} %bitcast.7, bf16[2048,256]{1,0:T(8,128)(2,1)} %wk_hbm.1, bf16[2048,256]{1,0:T(8,128)(2,1)} %wv_hbm.1), custom_call_target="tpu_custom_call" | custom-call | flops 1 | bytes 1 | tf_op jit(solution)/shard_map/pallas_call | solution.py:107
  5.4 6.4 %all-to-all-start = ((bf16[8,128,512]{2,1,0:T(8,128)(2,1)}), bf16[8,128,512]{2,1,0:T(8,128)(2,1)}, u32[]{:S(2)}, u32[]{:S(2)}) async-start(bf16[8,128,512]{2,1,0:T(8,128)(2,1)} %bitcast.6), calls=%async_computation | async-start | bytes 2097152 | tf_op jit(solution)/shard_map/all_to_all | solution.py:361
  11.8 7.5 %shard_map.59 = (bf16[1024,1024]{1,0:T(8,128)(2,1)S(1)}, bf16[128,1024]{1,0:T(8,128)(2,1)}, bf16[128,1024]{1,0:T(8,128)(2,1)}, bf16[128,1024]{1,0:T(8,128)(2,1)}...) custom-call(bf16[1024,2048]{1,0:T(8,128)(2,1)} %bitcast.8, ...), custom_call_target="tpu_custom_call" | custom-call | flops 1 | bytes 1 | tf_op jit(solution)/shard_map/pallas_call | solution.py:146
  19.2 1.4 %collective-permute-start.1 = (bf16[128,1024]{1,0:T(8,128)(2,1)}, bf16[128,1024]{1,0:T(8,128)(2,1)}, u32[]{:S(2)}, u32[]{:S(2)}) collective-permute-start(bf16[128,1024]{1,0:T(8,128)(2,1)} %get-tuple-element.23), channel_id=1, source_target_pairs={{28,24},{29,25},{30,26},{31,27}} | collective-permute-start | bytes 786440 | tf_op jit(solution)/shard_map/ppermute | solution.py:358
  20.6 0.7 %collective-permute-start.3 = (bf16[128,1024]{1,0:T(8,128)(2,1)}, bf16[128,1024]{1,0:T(8,128)(2,1)S(1)}, u32[]{:S(2)}, u32[]{:S(2)}) collective-permute-start(bf16[128,1024]{1,0:T(8,128)(2,1)} %get-tuple-element.26), channel_id=1, source_target_pairs={{28,0},{29,1},{30,2},{31,3}} | collective-permute-start | bytes 786440 | tf_op jit(solution)/shard_map/ppermute | solution.py:358
  21.3 1.3 %collective-permute-start.4 = (bf16[128,1024]{1,0:T(8,128)(2,1)}, bf16[128,1024]{1,0:T(8,128)(2,1)}, u32[]{:S(2)}, u32[]{:S(2)}) collective-permute-start(bf16[128,1024]{1,0:T(8,128)(2,1)} %get-tuple-element.27), channel_id=1, source_target_pairs={{28,4},{29,5},{30,6},{31,7}} | collective-permute-start | bytes 786440 | tf_op jit(solution)/shard_map/ppermute | solution.py:358
  22.6 1.4 %collective-permute-start.5 = (bf16[128,1024]{1,0:T(8,128)(2,1)}, bf16[128,1024]{1,0:T(8,128)(2,1)}, u32[]{:S(2)}, u32[]{:S(2)}) collective-permute-start(bf16[128,1024]{1,0:T(8,128)(2,1)} %get-tuple-element.29), channel_id=1, source_target_pairs={{28,24},{29,25},{30,26},{31,27}} | collective-permute-start | bytes 786440 | tf_op jit(solution)/shard_map/ppermute | solution.py:358
  24.0 0.0 collective-permute-start
  24.0 3.0 %shard_map.61 = (bf16[1024,1024]{1,0:T(8,128)(2,1)}, bf16[16,128]{1,0:T(8,128)(2,1)S(1)}) custom-call(s32[1]{0:T(128)} %bitcast.first_ref, bf16[1024,1024]{1,0:T(8,128)(2,1)S(1)} %get-tuple-element.17.q_ref.refs_0_, bf16[1024,512]{1,0:T(8,128)(2,1)S(1)} %copy-done), custom_call_target="tpu_custom_call" | custom-call | flops 1 | bytes 1 | tf_op jit(solution)/shard_map/pallas_call | solution.py:269
  27.0 0.0 collective-permute-done.1.b_hbm
  27.0 1.7 %shard_map.63 = bf16[128,1024]{1,0:T(8,128)(2,1)} custom-call(s32[1]{0:T(128)} %bitcast.2.which_ref, bf16[128,1024]{1,0:T(8,128)(2,1)} %get-tuple-element.22.a_hbm, bf16[128,1024]{1,0:T(8,128)(2,1)} %collective-permute-done.1.b_hbm, bf16[16,128]{1,0:T(8,128)(2,1)S(1)} %get-tuple-element.24.refs_0_), custom_call_target="tpu_custom_call" | custom-call | flops 1 | bytes 1 | tf_op jit(solution)/shard_map/pallas_call | solution.py:190
  28.7 1.4 %collective-permute-start.2 = (bf16[128,1024]{1,0:T(8,128)(2,1)}, bf16[128,1024]{1,0:T(8,128)(2,1)}, u32[]{:S(2)}, u32[]{:S(2)}) collective-permute-start(bf16[128,1024]{1,0:T(8,128)(2,1)} %shard_map.63), channel_id=1, source_target_pairs={{24,8},{28,12},{25,9},{29,13},{26,10},{30,14},{27,11},{31,15}} | collective-permute-start | bytes 786440 | tf_op jit(solution)/shard_map/ppermute | solution.py:358
  30.1 3.0 %shard_map.62 = (bf16[1024,1024]{1,0:T(8,128)(2,1)}, bf16[16,128]{1,0:T(8,128)(2,1)S(1)}) custom-call(s32[1]{0:T(128)} %bitcast.first_ref, bf16[1024,1024]{1,0:T(8,128)(2,1)S(1)} %get-tuple-element.17.q_ref.refs_0_, bf16[1024,512]{1,0:T(8,128)(2,1)S(1)} %copy-done, bf16[1024,1024]{1,0:T(8,128)(2,1)} %get-tuple-element.20.refs_0_), custom_call_target="tpu_custom_call", output_to_operand_aliasing={{0}: (3, {})} | custom-call | flops 1 | bytes 1 | tf_op jit(solution)/shard_map/pallas_call | solution.py:269
  33.1 0.0 collective-permute-done.3.refs_1_
  33.1 11.9 %collective-permute-done.4.refs_2_ = bf16[128,1024]{1,0:T(8,128)(2,1)} collective-permute-done((bf16[128,1024]{1,0:T(8,128)(2,1)}, bf16[128,1024]{1,0:T(8,128)(2,1)}, u32[]{:S(2)}, u32[]{:S(2)}) %collective-permute-start.4) | collective-permute-done | bytes 262176 | tf_op jit(solution)/shard_map/ppermute | solution.py:358
  45.0 0.0 collective-permute-done.5.b_hbm
  45.0 1.7 %shard_map.65.refs_1_ = bf16[128,1024]{1,0:T(8,128)(2,1)} custom-call(s32[1]{0:T(128)} %bitcast.2.which_ref, bf16[128,1024]{1,0:T(8,128)(2,1)} %get-tuple-element.28.a_hbm, bf16[128,1024]{1,0:T(8,128)(2,1)} %collective-permute-done.5.b_hbm, bf16[16,128]{1,0:T(8,128)(2,1)S(1)} %get-tuple-element.30.refs_0_, ...), custom_call_target="tpu_custom_call" | custom-call | flops 1 | bytes 1 | tf_op jit(solution)/shard_map/pallas_call | solution.py:190
  46.7 1.4 %collective-permute-start.6 = (bf16[128,1024]{1,0:T(8,128)(2,1)}, bf16[128,1024]{1,0:T(8,128)(2,1)}, u32[]{:S(2)}, u32[]{:S(2)}) collective-permute-start(bf16[128,1024]{1,0:T(8,128)(2,1)} %shard_map.65.refs_1_), channel_id=1, source_target_pairs={{24,16},{28,20},{25,17},{29,21},{26,18},{30,22},{27,19},{31,23}} | collective-permute-start | bytes 786440 | tf_op jit(solution)/shard_map/ppermute | solution.py:358
  48.1 1.3 %collective-permute-start.7 = (bf16[128,1024]{1,0:T(8,128)(2,1)}, bf16[128,1024]{1,0:T(8,128)(2,1)}, u32[]{:S(2)}, u32[]{:S(2)}) collective-permute-start(bf16[128,1024]{1,0:T(8,128)(2,1)} %shard_map.66), channel_id=1, source_target_pairs={{28,24},{29,25},{30,26},{31,27}} | collective-permute-start | bytes 786440 | tf_op jit(solution)/shard_map/ppermute | solution.py:358
  49.4 3.9 %shard_map.64 = (bf16[1024,1024]{1,0:T(8,128)(2,1)}, bf16[16,128]{1,0:T(8,128)(2,1)}) custom-call(s32[1]{0:T(128)} %bitcast.first_ref, bf16[1024,1024]{1,0:T(8,128)(2,1)S(1)} %get-tuple-element.17.q_ref.refs_0_, bf16[1024,512]{1,0:T(8,128)(2,1)S(1)} %copy-done, bf16[256,512]{1,0:T(8,128)(2,1)} %collective-permute-done.refs_0_, ...), custom_call_target="tpu_custom_call", output_to_operand_aliasing={{0}: (4, {})} | custom-call | flops 1000000000 | bytes 1 | tf_op jit(solution)/shard_map/pallas_call | solution.py:269
  53.3 0.0 collective-permute-done.6.refs_4_
  53.3 0.0 collective-permute-done.7.refs_5_
  53.3 0.6 all-to-all-done.refs_6_
  53.9 3.6 %shard_map.67 = bf16[128,1024]{1,0:T(8,128)(2,1)} custom-call(s32[1]{0:T(128)} %bitcast.4.which_ref, bf16[1024,1024]{1,0:T(8,128)(2,1)S(1)} %get-tuple-element.17.q_ref.refs_0_, bf16[128,1024]{1,0:T(8,128)(2,1)} %copy-done.1, bf16[128,1024]{1,0:T(8,128)(2,1)} %collective-permute-done.4.refs_2_, bf16[128,1024]{1,0:T(8,128)(2,1)} %collective-permute-done.2.refs_2_.refs_3_, ...), custom_call_target="tpu_custom_call" | custom-call | flops 1 | bytes 1 | tf_op jit(solution)/shard_map/pallas_call | solution.py:324
  (7 shorter events, 0.0 us)
Async XLA Ops:
  5.4 48.5 %all-to-all-start = ((bf16[8,128,512]{2,1,0:T(8,128)(2,1)}), bf16[8,128,512]{2,1,0:T(8,128)(2,1)}, u32[]{:S(2)}, u32[]{:S(2)}) async-start(bf16[8,128,512]{2,1,0:T(8,128)(2,1)} %bitcast.6), calls=%async_computation | async-start | bytes 2097152 | tf_op jit(solution)/shard_map/all_to_all | solution.py:361
  11.8 12.2 %copy-start = (bf16[1024,512]{1,0:T(8,128)(2,1)S(1)}, bf16[1024,512]{1,0:T(8,128)(2,1)}, u32[]{:S(2)}) copy-start(bf16[1024,512]{1,0:T(8,128)(2,1)} %get-tuple-element.18.kv_ref) | copy-start | bytes 3145732
  19.2 7.8 %collective-permute-start.1 = (bf16[128,1024]{1,0:T(8,128)(2,1)}, bf16[128,1024]{1,0:T(8,128)(2,1)}, u32[]{:S(2)}, u32[]{:S(2)}) collective-permute-start(bf16[128,1024]{1,0:T(8,128)(2,1)} %get-tuple-element.23), channel_id=1, source_target_pairs={{28,24},{29,25},{30,26},{31,27}} | collective-permute-start | bytes 786440 | tf_op jit(solution)/shard_map/ppermute | solution.py:358
  20.6 12.4 %collective-permute-start.3 = (bf16[128,1024]{1,0:T(8,128)(2,1)}, bf16[128,1024]{1,0:T(8,128)(2,1)S(1)}, u32[]{:S(2)}, u32[]{:S(2)}) collective-permute-start(bf16[128,1024]{1,0:T(8,128)(2,1)} %get-tuple-element.26), channel_id=1, source_target_pairs={{28,0},{29,1},{30,2},{31,3}} | collective-permute-start | bytes 786440 | tf_op jit(solution)/shard_map/ppermute | solution.py:358
  21.3 23.7 %collective-permute-start.4 = (bf16[128,1024]{1,0:T(8,128)(2,1)}, bf16[128,1024]{1,0:T(8,128)(2,1)}, u32[]{:S(2)}, u32[]{:S(2)}) collective-permute-start(bf16[128,1024]{1,0:T(8,128)(2,1)} %get-tuple-element.27), channel_id=1, source_target_pairs={{28,4},{29,5},{30,6},{31,7}} | collective-permute-start | bytes 786440 | tf_op jit(solution)/shard_map/ppermute | solution.py:358
  22.6 22.4 %collective-permute-start.5 = (bf16[128,1024]{1,0:T(8,128)(2,1)}, bf16[128,1024]{1,0:T(8,128)(2,1)}, u32[]{:S(2)}, u32[]{:S(2)}) collective-permute-start(bf16[128,1024]{1,0:T(8,128)(2,1)} %get-tuple-element.29), channel_id=1, source_target_pairs={{28,24},{29,25},{30,26},{31,27}} | collective-permute-start | bytes 786440 | tf_op jit(solution)/shard_map/ppermute | solution.py:358
  24.0 25.4 %collective-permute-start = (bf16[256,512]{1,0:T(8,128)(2,1)}, bf16[256,512]{1,0:T(8,128)(2,1)}, u32[]{:S(2)}, u32[]{:S(2)}) collective-permute-start(bf16[256,512]{1,0:T(8,128)(2,1)} %get-tuple-element.19), channel_id=1, source_target_pairs={{0,1},{1,2},{2,3},{3,0},{4,5},{5,6},{6,7},{7,4},{8,9},{9,10},{10,1... | collective-permute-start | bytes 786440 | tf_op jit(solution)/shard_map/ppermute | solution.py:362
  28.7 20.7 %collective-permute-start.2 = (bf16[128,1024]{1,0:T(8,128)(2,1)}, bf16[128,1024]{1,0:T(8,128)(2,1)}, u32[]{:S(2)}, u32[]{:S(2)}) collective-permute-start(bf16[128,1024]{1,0:T(8,128)(2,1)} %shard_map.63), channel_id=1, source_target_pairs={{24,8},{28,12},{25,9},{29,13},{26,10},{30,14},{27,11},{31,15}} | collective-permute-start | bytes 786440 | tf_op jit(solution)/shard_map/ppermute | solution.py:358
  33.1 20.2 %copy-start.1 = (bf16[128,1024]{1,0:T(8,128)(2,1)}, bf16[128,1024]{1,0:T(8,128)(2,1)S(1)}, u32[]{:S(2)}) copy-start(bf16[128,1024]{1,0:T(8,128)(2,1)S(1)} %collective-permute-done.3.refs_1_) | copy-start | bytes 786436
  46.7 6.6 %collective-permute-start.6 = (bf16[128,1024]{1,0:T(8,128)(2,1)}, bf16[128,1024]{1,0:T(8,128)(2,1)}, u32[]{:S(2)}, u32[]{:S(2)}) collective-permute-start(bf16[128,1024]{1,0:T(8,128)(2,1)} %shard_map.65.refs_1_), channel_id=1, source_target_pairs={{24,16},{28,20},{25,17},{29,21},{26,18},{30,22},{27,19},{31,23}} | collective-permute-start | bytes 786440 | tf_op jit(solution)/shard_map/ppermute | solution.py:358
  48.1 5.3 %collective-permute-start.7 = (bf16[128,1024]{1,0:T(8,128)(2,1)}, bf16[128,1024]{1,0:T(8,128)(2,1)}, u32[]{:S(2)}, u32[]{:S(2)}) collective-permute-start(bf16[128,1024]{1,0:T(8,128)(2,1)} %shard_map.66), channel_id=1, source_target_pairs={{28,24},{29,25},{30,26},{31,27}} | collective-permute-start | bytes 786440 | tf_op jit(solution)/shard_map/ppermute | solution.py:358

commit v4 on v3

--- a/solution.py
+++ b/solution.py
@@ -18,6 +18,7 @@
 RELAYS = 2
 LAST_FLOPS = 10**9
 PIECES = 4
+BAND_LAST = 3
 LAST_ROWS = 256
 MIB = 1024 * 1024
 VMEM = pl.BlockSpec(memory_space=pltpu.VMEM)
@@ -349,39 +350,47 @@
     part = rows // steps
     shards = lax.axis_size("tok")
     root, buddy = steps - 1, steps - 2
-    first = flag(lax.axis_index("tok") == 0)
-    is_root = flag(here == root)
-    by_buddy = list(range(0, buddy, 2))[-RELAYS:]
-    straight = [i for i in range(buddy) if i // 2 * 2 not in by_buddy]
-
-    def send(block, *pairs):
-        return lax.ppermute(block, "depth", list(pairs))
+    shard = lax.axis_index("tok")
+    first, is_root, both = flag(shard == 0), flag(here == root), range(2)
+    even = list(range(0, buddy, 2))
+    by_buddy, split = even[:RELAYS], even[RELAYS : RELAYS + 1]
+    straight = [i for i in range(buddy) if i // 2 * 2 not in by_buddy and i not in split]
+
+    def send(block, *moves):
+        pairs = [tuple(step * shards + t for step in pair) for t in range(shards) for pair in moves[t % len(moves)]]
+        return lax.ppermute(block, ("depth", "tok"), pairs)
 
     kv, rim = project_kv(local, w_key, w_value)
     spread = lax.all_to_all(kv.reshape(steps, part, kv.shape[1]), "depth", split_axis=0, concat_axis=0, tiled=True)
     rim = lax.ppermute(rim, "tok", [(t, (t + 1) % shards) for t in range(shards)])
     query, *queries = project_q(local, w_query, steps)
 
-    relayed = [send(queries[index], (root, buddy)) for index in by_buddy]
-    direct = [send(queries[index], (root, index)) for index in straight]
+    relayed = [send(queries[index], [(root, buddy)]) for index in by_buddy]
+    halved = [send(queries[index], [(root, buddy)], [(root, index)]) for index in split]
+    direct = [send(queries[index], [(root, index)]) for index in straight]
+    cases = direct + halved
+    owners = [[(i, p) for p in both] for i in straight] + [[(i, 1)] for i in split]
     blocks = list(range(rows // BAND))
-    calls = len(by_buddy) + 1
-    window_out, after, beside = None, [], []
-    for turn in range(calls):
-        low, high = len(blocks) * (calls - 1 - turn) // calls, len(blocks) * (calls - turn) // calls
-        flops = LAST_FLOPS if turn == calls - 1 else 1
-        window_out, token = band_attend(first, query, kv, rim, blocks[low:high], window_out, after, flops)
-        if turn < calls - 1:
-            index = by_buddy[turn]
-            last = turn == calls - 2
-            block = choose(is_root, queries[index + 1], relayed[turn], [token] + (direct if last else []))
-            if last:
-                after = list(beside)
-            beside.append(send(block, (buddy, index), (root, index + 1)))
-    own = send(once(queries[buddy], [block]), (root, buddy))
-    owners = [[i] for i in straight] + [[i, i + 1] for i in by_buddy] + [[buddy]]
-    which = sum((jnp.where(here == i, case + 1, 0) for case, ends in enumerate(owners) for i in ends), 0)
-    depth_out = depth_attend(flag(which), query, direct + beside + [own], spread)
+    high = len(blocks) * BAND_LAST // 8
+    window_out, token = band_attend(first, query, kv, rim, blocks[high:], None, [])
+    beside = []
+    for index, got in zip(by_buddy, relayed):
+        waits = [token] + (direct if index == by_buddy[-1] else [])
+        block = choose(is_root, queries[index + 1], got, waits)
+        first_block = block if not beside else first_block
+        beside.append(send(block, [(buddy, index), (root, index + 1)]))
+        owners.append([(i, p) for i in (index, index + 1) for p in both])
+    own = once(queries[buddy], [first_block])
+    cases += beside + [send(own, [(root, buddy)])]
+    owners.append([(buddy, p) for p in both])
+    for index, half in zip(split, halved):
+        cases.append(send(half, [(buddy, index)], []))
+        owners.append([(index, 0)])
+    window_out, _ = band_attend(first, query, kv, rim, blocks[:high], window_out, beside[:-1], LAST_FLOPS)
+    which = sum(
+        (jnp.where((here == i) & (shard % 2 == p), case + 1, 0) for case, ends in enumerate(owners) for i, p in ends), 0
+    )
+    depth_out = depth_attend(flag(which), query, cases, spread)
     return (window_out[None], depth_out)
 
 

time: 57.8 us -> 55.7 us (0.964)
  the two profiles are of different devices: /device:TPU:2 before, /device:TPU:16 now
where the time goes in v4:
time: 55.7 us; the launch traced here: 55.3 us
  Pallas kernels  28.2 us (51%)
  starting transfers between devices  16.4 us (29%)
  waiting for transfers between devices  9.86 us (18%)
  between operations  0.87 us (2%)
    ppermute x8, starting transfers between devices, send(): return lax.ppermute(block, ('depth', 'tok'), pairs)  10.2 us
    ppermute x8, waiting for transfers between devices, send(): return lax.ppermute(block, ('depth', 'tok'), pairs)  9.85 us
    pallas_call x2, Pallas kernels, band_attend(): pl.pallas_call(functools.partial(band_kernel, blocks_of), out_shape=[arra...  9.04 us
    pallas_call x1, Pallas kernels, project_q(): pl.pallas_call(functools.partial(project_q_kernel, part), out_shape=[arra...  7.48 us
    all_to_all x1, starting transfers between devices, body(): lax.all_to_all(kv.reshape(steps, part, kv.shape[1]), 'depth', split_axis=...  6.15 us
    pallas_call x1, Pallas kernels, project_kv(): pl.pallas_call(project_kv_kernel, out_shape=[hbm_array(count, 2 * width),...  4.78 us
    pallas_call x1, Pallas kernels, depth_attend(): pl.pallas_call(functools.partial(depth_kernel, 1 + len(queries)), out_sha...  3.59 us
    pallas_call x2, Pallas kernels, choose(): pl.pallas_call(choose_kernel, out_shape=array(*a.shape), in_specs=[SMEM]...  3.31 us
  transfers between devices with their start and end apart: 10, of which 1 were waited for; matrix products, arithmetic and copies ran while one was open for 0% of the time, Pallas kernels for 36%

profile of v4, /device:TPU:16, one launch (start us, length us, event | category | flops | bytes accessed | tf_op | source)
XLA Modules:
  0.0 55.3 jit_solution(16558862252731817026)
XLA Ops:
  0.6 4.8 %shard_map.60 = (bf16[1024,512]{1,0:T(8,128)(2,1)}, bf16[256,512]{1,0:T(8,128)(2,1)}) custom-call(bf16[1024,2048]{1,0:T(8,128)(2,1)} %bitcast.7, bf16[2048,256]{1,0:T(8,128)(2,1)} %wk_hbm.1, bf16[2048,256]{1,0:T(8,128)(2,1)} %wv_hbm.1), custom_call_target="tpu_custom_call" | custom-call | flops 1 | bytes 1 | tf_op jit(solution)/shard_map/pallas_call | solution.py:108
  5.4 6.1 %all-to-all-start = ((bf16[8,128,512]{2,1,0:T(8,128)(2,1)}), bf16[8,128,512]{2,1,0:T(8,128)(2,1)}, u32[]{:S(2)}, u32[]{:S(2)}) async-start(bf16[8,128,512]{2,1,0:T(8,128)(2,1)} %bitcast.6), calls=%async_computation | async-start | bytes 2097152 | tf_op jit(solution)/shard_map/all_to_all | solution.py:364
  11.6 7.5 %shard_map.59 = (bf16[1024,1024]{1,0:T(8,128)(2,1)S(1)}, bf16[128,1024]{1,0:T(8,128)(2,1)}, bf16[128,1024]{1,0:T(8,128)(2,1)}, bf16[128,1024]{1,0:T(8,128)(2,1)}...) custom-call(bf16[1024,2048]{1,0:T(8,128)(2,1)} %bitcast.8, ...), custom_call_target="tpu_custom_call" | custom-call | flops 1 | bytes 1 | tf_op jit(solution)/shard_map/pallas_call | solution.py:147
  19.1 1.4 %collective-permute-start.1 = (bf16[128,1024]{1,0:T(8,128)(2,1)}, bf16[128,1024]{1,0:T(8,128)(2,1)}, u32[]{:S(2)}, u32[]{:S(2)}) collective-permute-start(bf16[128,1024]{1,0:T(8,128)(2,1)} %get-tuple-element.20), channel_id=1, source_target_pairs={{28,24},{29,25},{30,26},{31,27}} | collective-permute-start | bytes 786440 | tf_op jit(solution)/shard_map/ppermute | solution.py:361
  20.5 1.4 %collective-permute-start.3 = (bf16[128,1024]{1,0:T(8,128)(2,1)}, bf16[128,1024]{1,0:T(8,128)(2,1)}, u32[]{:S(2)}, u32[]{:S(2)}) collective-permute-start(bf16[128,1024]{1,0:T(8,128)(2,1)} %get-tuple-element.23), channel_id=1, source_target_pairs={{28,20},{29,21},{30,22},{31,23}} | collective-permute-start | bytes 786440 | tf_op jit(solution)/shard_map/ppermute | solution.py:361
  21.8 1.4 %collective-permute-start.5 = (bf16[128,1024]{1,0:T(8,128)(2,1)}, bf16[128,1024]{1,0:T(8,128)(2,1)}, u32[]{:S(2)}, u32[]{:S(2)}) collective-permute-start(bf16[128,1024]{1,0:T(8,128)(2,1)} %get-tuple-element.26), channel_id=1, source_target_pairs={{28,24},{29,25},{30,26},{31,27}} | collective-permute-start | bytes 786440 | tf_op jit(solution)/shard_map/ppermute | solution.py:361
  23.2 1.4 %collective-permute-start.4 = (bf16[128,1024]{1,0:T(8,128)(2,1)}, bf16[128,1024]{1,0:T(8,128)(2,1)}, u32[]{:S(2)}, u32[]{:S(2)}) collective-permute-start(bf16[128,1024]{1,0:T(8,128)(2,1)} %get-tuple-element.24), channel_id=1, source_target_pairs={{28,24},{29,17},{30,26},{31,19}} | collective-permute-start | bytes 786440 | tf_op jit(solution)/shard_map/ppermute | solution.py:361
  24.6 0.0 collective-permute-start
  24.6 4.4 %shard_map.61 = (bf16[1024,1024]{1,0:T(8,128)(2,1)}, bf16[16,128]{1,0:T(8,128)(2,1)S(1)}) custom-call(s32[1]{0:T(128)} %bitcast.first_ref, bf16[1024,1024]{1,0:T(8,128)(2,1)S(1)} %get-tuple-element.15.q_ref.refs_0_, bf16[1024,512]{1,0:T(8,128)(2,1)S(1)} %copy-done), custom_call_target="tpu_custom_call" | custom-call | flops 1 | bytes 1 | tf_op jit(solution)/shard_map/pallas_call | solution.py:270
  29.0 0.0 collective-permute-done.1.b_hbm
  29.0 1.7 %shard_map.62.refs_1_ = bf16[128,1024]{1,0:T(8,128)(2,1)} custom-call(s32[1]{0:T(128)} %bitcast.2.which_ref, bf16[128,1024]{1,0:T(8,128)(2,1)} %get-tuple-element.19.a_hbm, bf16[128,1024]{1,0:T(8,128)(2,1)} %collective-permute-done.1.b_hbm, bf16[16,128]{1,0:T(8,128)(2,1)S(1)} %get-tuple-element.21.refs_0_), custom_call_target="tpu_custom_call" | custom-call | flops 1 | bytes 1 | tf_op jit(solution)/shard_map/pallas_call | solution.py:191
  30.6 0.7 %collective-permute-start.2 = (bf16[128,1024]{1,0:T(8,128)(2,1)}, bf16[128,1024]{1,0:T(8,128)(2,1)S(1)}, u32[]{:S(2)}, u32[]{:S(2)}) collective-permute-start(bf16[128,1024]{1,0:T(8,128)(2,1)} %shard_map.62.refs_1_), channel_id=1, source_target_pairs={{24,0},{28,4},{25,1},{29,5},{26,2},{30,6},{27,3},{31,7}} | collective-permute-start | bytes 786440 | tf_op jit(solution)/shard_map/ppermute | solution.py:361
  31.4 1.4 %collective-permute-start.7 = (bf16[128,1024]{1,0:T(8,128)(2,1)}, bf16[128,1024]{1,0:T(8,128)(2,1)}, u32[]{:S(2)}, u32[]{:S(2)}) collective-permute-start(bf16[128,1024]{1,0:T(8,128)(2,1)} %shard_map.65), channel_id=1, source_target_pairs={{28,24},{29,25},{30,26},{31,27}} | collective-permute-start | bytes 786440 | tf_op jit(solution)/shard_map/ppermute | solution.py:361
  32.7 0.0 collective-permute-done.5.b_hbm
  32.7 1.6 %shard_map.64 = bf16[128,1024]{1,0:T(8,128)(2,1)} custom-call(s32[1]{0:T(128)} %bitcast.2.which_ref, bf16[128,1024]{1,0:T(8,128)(2,1)} %get-tuple-element.25.a_hbm, bf16[128,1024]{1,0:T(8,128)(2,1)} %collective-permute-done.5.b_hbm, bf16[16,128]{1,0:T(8,128)(2,1)S(1)} %get-tuple-element.21.refs_0_, bf16[128,1024]{1,0:T(8,128)(2,1)} %collective-permute-done.3.refs_1_), custom_call_target="tpu_custom_call" | custom-call | flops 1 | bytes 1 | tf_op jit(solution)/shard_map/pallas_call | solution.py:191
  34.4 1.4 %collective-permute-start.6 = (bf16[128,1024]{1,0:T(8,128)(2,1)}, bf16[128,1024]{1,0:T(8,128)(2,1)}, u32[]{:S(2)}, u32[]{:S(2)}) collective-permute-start(bf16[128,1024]{1,0:T(8,128)(2,1)} %shard_map.64), channel_id=1, source_target_pairs={{24,8},{28,12},{25,9},{29,13},{26,10},{30,14},{27,11},{31,15}} | collective-permute-start | bytes 786440 | tf_op jit(solution)/shard_map/ppermute | solution.py:361
  35.7 0.0 collective-permute-done.4.refs_2_
  35.8 1.3 %collective-permute-start.8 = (bf16[128,1024]{1,0:T(8,128)(2,1)}, bf16[128,1024]{1,0:T(8,128)(2,1)}, u32[]{:S(2)}, u32[]{:S(2)}) collective-permute-start(bf16[128,1024]{1,0:T(8,128)(2,1)} %collective-permute-done.4.refs_2_), channel_id=1, source_target_pairs={{24,16},{26,18}} | collective-permute-start | bytes 786440 | tf_op jit(solution)/shard_map/ppermute | solution.py:361
  37.1 0.0 collective-permute-done.2.refs_2_.refs_3_
  37.2 4.7 %shard_map.63 = (bf16[1024,1024]{1,0:T(8,128)(2,1)}, bf16[16,128]{1,0:T(8,128)(2,1)}) custom-call(s32[1]{0:T(128)} %bitcast.first_ref, bf16[1024,1024]{1,0:T(8,128)(2,1)S(1)} %get-tuple-element.15.q_ref.refs_0_, bf16[1024,512]{1,0:T(8,128)(2,1)S(1)} %copy-done, bf16[256,512]{1,0:T(8,128)(2,1)} %collective-permute-done.refs_0_, ...), custom_call_target="tpu_custom_call", output_to_operand_aliasing={{0}: (4, {})} | custom-call | flops 1000000000 | bytes 1 | tf_op jit(solution)/shard_map/pallas_call | solution.py:270
  41.9 0.0 collective-permute-done.7.refs_5_
  41.9 9.8 %collective-permute-done.8.refs_6_ = bf16[128,1024]{1,0:T(8,128)(2,1)} collective-permute-done((bf16[128,1024]{1,0:T(8,128)(2,1)}, bf16[128,1024]{1,0:T(8,128)(2,1)}, u32[]{:S(2)}, u32[]{:S(2)}) %collective-permute-start.8) | collective-permute-done | bytes 262176 | tf_op jit(solution)/shard_map/ppermute | solution.py:361
  51.7 0.0 all-to-all-done.refs_7_
  51.7 3.6 %shard_map.66 = bf16[128,1024]{1,0:T(8,128)(2,1)} custom-call(s32[1]{0:T(128)} %bitcast.4.which_ref, bf16[1024,1024]{1,0:T(8,128)(2,1)S(1)} %get-tuple-element.15.q_ref.refs_0_, bf16[128,1024]{1,0:T(8,128)(2,1)} %collective-permute-done.3.refs_1_, bf16[128,1024]{1,0:T(8,128)(2,1)} %collective-permute-done.4.refs_2_, bf16[128,1024]{1,0:T(8,128)(2,1)} %copy-done.1, ...), custom_call_target="tpu_custom_call" | custom-call | flops 1 | bytes 1 | tf_op jit(solution)/shard_map/pallas_call | solution.py:325
  (8 shorter events, 0.0 us)
Async XLA Ops:
  5.4 46.3 %all-to-all-start = ((bf16[8,128,512]{2,1,0:T(8,128)(2,1)}), bf16[8,128,512]{2,1,0:T(8,128)(2,1)}, u32[]{:S(2)}, u32[]{:S(2)}) async-start(bf16[8,128,512]{2,1,0:T(8,128)(2,1)} %bitcast.6), calls=%async_computation | async-start | bytes 2097152 | tf_op jit(solution)/shard_map/all_to_all | solution.py:364
  11.6 13.0 %copy-start = (bf16[1024,512]{1,0:T(8,128)(2,1)S(1)}, bf16[1024,512]{1,0:T(8,128)(2,1)}, u32[]{:S(2)}) copy-start(bf16[1024,512]{1,0:T(8,128)(2,1)} %get-tuple-element.16.kv_ref) | copy-start | bytes 3145732
  19.1 9.9 %collective-permute-start.1 = (bf16[128,1024]{1,0:T(8,128)(2,1)}, bf16[128,1024]{1,0:T(8,128)(2,1)}, u32[]{:S(2)}, u32[]{:S(2)}) collective-permute-start(bf16[128,1024]{1,0:T(8,128)(2,1)} %get-tuple-element.20), channel_id=1, source_target_pairs={{28,24},{29,25},{30,26},{31,27}} | collective-permute-start | bytes 786440 | tf_op jit(solution)/shard_map/ppermute | solution.py:361
  20.5 10.9 %collective-permute-start.3 = (bf16[128,1024]{1,0:T(8,128)(2,1)}, bf16[128,1024]{1,0:T(8,128)(2,1)}, u32[]{:S(2)}, u32[]{:S(2)}) collective-permute-start(bf16[128,1024]{1,0:T(8,128)(2,1)} %get-tuple-element.23), channel_id=1, source_target_pairs={{28,20},{29,21},{30,22},{31,23}} | collective-permute-start | bytes 786440 | tf_op jit(solution)/shard_map/ppermute | solution.py:361
  21.8 10.9 %collective-permute-start.5 = (bf16[128,1024]{1,0:T(8,128)(2,1)}, bf16[128,1024]{1,0:T(8,128)(2,1)}, u32[]{:S(2)}, u32[]{:S(2)}) collective-permute-start(bf16[128,1024]{1,0:T(8,128)(2,1)} %get-tuple-element.26), channel_id=1, source_target_pairs={{28,24},{29,25},{30,26},{31,27}} | collective-permute-start | bytes 786440 | tf_op jit(solution)/shard_map/ppermute | solution.py:361
  23.2 12.6 %collective-permute-start.4 = (bf16[128,1024]{1,0:T(8,128)(2,1)}, bf16[128,1024]{1,0:T(8,128)(2,1)}, u32[]{:S(2)}, u32[]{:S(2)}) collective-permute-start(bf16[128,1024]{1,0:T(8,128)(2,1)} %get-tuple-element.24), channel_id=1, source_target_pairs={{28,24},{29,17},{30,26},{31,19}} | collective-permute-start | bytes 786440 | tf_op jit(solution)/shard_map/ppermute | solution.py:361
  24.6 12.6 %collective-permute-start = (bf16[256,512]{1,0:T(8,128)(2,1)}, bf16[256,512]{1,0:T(8,128)(2,1)}, u32[]{:S(2)}, u32[]{:S(2)}) collective-permute-start(bf16[256,512]{1,0:T(8,128)(2,1)} %get-tuple-element.17), channel_id=1, source_target_pairs={{0,1},{1,2},{2,3},{3,0},{4,5},{5,6},{6,7},{7,4},{8,9},{9,10},{10,1... | collective-permute-start | bytes 786440 | tf_op jit(solution)/shard_map/ppermute | solution.py:365
  30.6 6.5 %collective-permute-start.2 = (bf16[128,1024]{1,0:T(8,128)(2,1)}, bf16[128,1024]{1,0:T(8,128)(2,1)S(1)}, u32[]{:S(2)}, u32[]{:S(2)}) collective-permute-start(bf16[128,1024]{1,0:T(8,128)(2,1)} %shard_map.62.refs_1_), channel_id=1, source_target_pairs={{24,0},{28,4},{25,1},{29,5},{26,2},{30,6},{27,3},{31,7}} | collective-permute-start | bytes 786440 | tf_op jit(solution)/shard_map/ppermute | solution.py:361
  31.4 10.5 %collective-permute-start.7 = (bf16[128,1024]{1,0:T(8,128)(2,1)}, bf16[128,1024]{1,0:T(8,128)(2,1)}, u32[]{:S(2)}, u32[]{:S(2)}) collective-permute-start(bf16[128,1024]{1,0:T(8,128)(2,1)} %shard_map.65), channel_id=1, source_target_pairs={{28,24},{29,25},{30,26},{31,27}} | collective-permute-start | bytes 786440 | tf_op jit(solution)/shard_map/ppermute | solution.py:361
  34.4 7.5 %collective-permute-start.6 = (bf16[128,1024]{1,0:T(8,128)(2,1)}, bf16[128,1024]{1,0:T(8,128)(2,1)}, u32[]{:S(2)}, u32[]{:S(2)}) collective-permute-start(bf16[128,1024]{1,0:T(8,128)(2,1)} %shard_map.64), channel_id=1, source_target_pairs={{24,8},{28,12},{25,9},{29,13},{26,10},{30,14},{27,11},{31,15}} | collective-permute-start | bytes 786440 | tf_op jit(solution)/shard_map/ppermute | solution.py:361
  35.8 16.0 %collective-permute-start.8 = (bf16[128,1024]{1,0:T(8,128)(2,1)}, bf16[128,1024]{1,0:T(8,128)(2,1)}, u32[]{:S(2)}, u32[]{:S(2)}) collective-permute-start(bf16[128,1024]{1,0:T(8,128)(2,1)} %collective-permute-done.4.refs_2_), channel_id=1, source_target_pairs={{24,16},{26,18}} | collective-permute-start | bytes 786440 | tf_op jit(solution)/shard_map/ppermute | solution.py:361
  37.2 4.7 %copy-start.1 = (bf16[128,1024]{1,0:T(8,128)(2,1)}, bf16[128,1024]{1,0:T(8,128)(2,1)S(1)}, u32[]{:S(2)}) copy-start(bf16[128,1024]{1,0:T(8,128)(2,1)S(1)} %collective-permute-done.2.refs_2_.refs_3_) | copy-start | bytes 786436

commit v5 on v4

--- a/solution.py
+++ b/solution.py
@@ -187,16 +187,42 @@
     pltpu.make_async_copy(b_hbm, out_ref, sem).wait()
 
 
+def nothing_kernel(*refs):
+    pass
+
+
+def once(block, arrays):
+    return pl.pallas_call(
+        nothing_kernel,
+        out_shape=hbm_array(*block.shape),
+        in_specs=[HBM] + [ANY] * len(arrays),
+        out_specs=HBM,
+        input_output_aliases={0: 0},
+        cost_estimate=cost(),
+    )(*in_hbm(block), *arrays)
+
+
+def choose_kernel(which_ref, a_hbm, b_hbm, *refs):
+    out_ref, sem = refs[-2:]
+    for flag, source in ((1, a_hbm), (0, b_hbm)):
+
+        @pl.when(which_ref[0] == flag)
+        def _(source=source):
+            pltpu.make_async_copy(source, out_ref, sem).start()
+
+    pltpu.make_async_copy(b_hbm, out_ref, sem).wait()
+
+
 def choose(which, a, b, after):
     return pl.pallas_call(
         choose_kernel,
-        out_shape=array(*a.shape),
-        in_specs=[SMEM] + [HBM] * 2 + [ANY] * len(after),
+        out_shape=buffer(*a.shape),
+        in_specs=[SMEM, HBM] + [ANY] * (1 + len(after)),
         out_specs=VMEM,
         scratch_shapes=[pltpu.SemaphoreType.DMA],
         compiler_params=params(16),
         cost_estimate=cost(),
-    )(which, *in_hbm(a, b), *after)
+    )(which, *in_hbm(a), b, *after)
 
 
 def band_kernel(blocks_of, first_ref, q_ref, kv_ref, *refs):
@@ -274,7 +300,7 @@
         out_specs=[ANY, VMEM],
         scratch_shapes=[buffer(rows, width), pltpu.SemaphoreType.DMA((len(blocks_of),))],
         input_output_aliases={3 + len(inside): 0} if given else {},
-        compiler_params=params(16),
+        compiler_params=params(10),
         cost_estimate=cost(flops),
     )(first, query, kv, *inside, *given, *after)
 
@@ -283,7 +309,7 @@
     q_hbms, (kv_hbm, out_hbm, q_ref, kv_ref, out_ref, sems) = refs[:cases], refs[cases:]
     steps, count, width = kv_ref.shape
     width //= 2
-    chunk = min(count, 32)
+    chunk = min(count, 64)
     chunks = [pl.ds(start, chunk) for start in range(0, count, chunk)]
     last = pl.ds(q_hbms[0].shape[0] - count, count)
     loads = []
@@ -325,17 +351,17 @@
     return pl.pallas_call(
         functools.partial(depth_kernel, 1 + len(queries)),
         out_shape=array(*shape),
-        in_specs=[SMEM, ANY] + [HBM] * len(queries) + [HBM],
+        in_specs=[SMEM, ANY] + [ANY] * len(queries) + [HBM],
         out_specs=ANY,
         scratch_shapes=[
             buffer(*shape),
             buffer(*kv.shape),
             buffer(*shape),
-            pltpu.SemaphoreType.DMA((1 + 2 * -(-count // min(count, 32)),)),
+            pltpu.SemaphoreType.DMA((1 + 2 * -(-count // min(count, 64)),)),
         ],
         compiler_params=params(16),
         cost_estimate=cost(),
-    )(which, query, *in_hbm(*queries, kv))
+    )(which, query, *queries, *in_hbm(kv))
 
 
 def flag(value):
@@ -354,7 +380,9 @@
     first, is_root, both = flag(shard == 0), flag(here == root), range(2)
     even = list(range(0, buddy, 2))
     by_buddy, split = even[:RELAYS], even[RELAYS : RELAYS + 1]
-    straight = [i for i in range(buddy) if i // 2 * 2 not in by_buddy and i not in split]
+    beside_of = {index: index + 1 for index in by_buddy}
+    beside_of.update(zip(by_buddy, range(buddy - 1 - 2 * (len(by_buddy) - 1), buddy, 2)))
+    straight = [i for i in range(1, buddy, 2) if i not in beside_of.values()] + even[RELAYS + 1 :]
 
     def send(block, *moves):
         pairs = [tuple(step * shards + t for step in pair) for t in range(shards) for pair in moves[t % len(moves)]]
@@ -376,10 +404,10 @@
     beside = []
     for index, got in zip(by_buddy, relayed):
         waits = [token] + (direct if index == by_buddy[-1] else [])
-        block = choose(is_root, queries[index + 1], got, waits)
+        block = choose(is_root, queries[beside_of[index]], got, waits)
         first_block = block if not beside else first_block
-        beside.append(send(block, [(buddy, index), (root, index + 1)]))
-        owners.append([(i, p) for i in (index, index + 1) for p in both])
+        beside.append(send(block, [(buddy, index), (root, beside_of[index])]))
+        owners.append([(i, p) for i in (index, beside_of[index]) for p in both])
     own = once(queries[buddy], [first_block])
     cases += beside + [send(own, [(root, buddy)])]
     owners.append([(buddy, p) for p in both])

time: 55.7 us -> 55.5 us (level)
  waiting for transfers between devices: 9.86 us -> 11.6 us
  Pallas kernels: 28.2 us -> 27.1 us
  starting transfers between devices: 16.4 us -> 15.7 us
    ppermute x8, waiting for transfers between devices: 9.85 us -> 11.5 us  [send(): return lax.ppermute(block, ('depth', 'tok'), pairs)]
    pallas_call x2, Pallas kernels: 3.31 us -> 2.38 us  [choose(): pl.pallas_call(choose_kernel, out_shape=buffer(*a.shape), in_specs=[SMEM,...]
    ppermute x8, starting transfers between devices: 10.2 us -> 9.52 us  [send(): return lax.ppermute(block, ('depth', 'tok'), pairs)]
  transfers between devices with their start and end apart: 10 -> 10, of which waited for: 1 -> 1; matrix products, arithmetic and copies ran while one was open for 0% -> 0% of each run, Pallas kernels for 36% -> 34%
where the time goes in v5:
time: 55.5 us; the launch traced here: 55.2 us
  Pallas kernels  27.1 us (49%)
  starting transfers between devices  15.7 us (28%)
  waiting for transfers between devices  11.6 us (21%)
  between operations  0.86 us (2%)
    ppermute x8, waiting for transfers between devices, send(): return lax.ppermute(block, ('depth', 'tok'), pairs)  11.5 us
    ppermute x8, starting transfers between devices, send(): return lax.ppermute(block, ('depth', 'tok'), pairs)  9.52 us
    pallas_call x2, Pallas kernels, band_attend(): pl.pallas_call(functools.partial(band_kernel, blocks_of), out_shape=[arra...  8.96 us
    pallas_call x1, Pallas kernels, project_q(): pl.pallas_call(functools.partial(project_q_kernel, part), out_shape=[arra...  7.48 us
    all_to_all x1, starting transfers between devices, body(): lax.all_to_all(kv.reshape(steps, part, kv.shape[1]), 'depth', split_axis=...  6.15 us
    pallas_call x1, Pallas kernels, project_kv(): pl.pallas_call(project_kv_kernel, out_shape=[hbm_array(count, 2 * width),...  4.78 us
    pallas_call x1, Pallas kernels, depth_attend(): pl.pallas_call(functools.partial(depth_kernel, 1 + len(queries)), out_sha...  3.46 us
    pallas_call x2, Pallas kernels, choose(): pl.pallas_call(choose_kernel, out_shape=buffer(*a.shape), in_specs=[SMEM,...  2.38 us
  transfers between devices with their start and end apart: 10, of which 1 were waited for; matrix products, arithmetic and copies ran while one was open for 0% of the time, Pallas kernels for 34%

profile of v5, /device:TPU:16, one launch (start us, length us, event | category | flops | bytes accessed | tf_op | source)
XLA Modules:
  0.0 55.2 jit_solution(968450836448906631)
XLA Ops:
  0.6 4.8 %shard_map.60 = (bf16[1024,512]{1,0:T(8,128)(2,1)}, bf16[256,512]{1,0:T(8,128)(2,1)}) custom-call(bf16[1024,2048]{1,0:T(8,128)(2,1)} %bitcast.7, bf16[2048,256]{1,0:T(8,128)(2,1)} %wk_hbm.1, bf16[2048,256]{1,0:T(8,128)(2,1)} %wv_hbm.1), custom_call_target="tpu_custom_call" | custom-call | flops 1 | bytes 1 | tf_op jit(solution)/shard_map/pallas_call | solution.py:108
  5.4 6.1 %all-to-all-start = ((bf16[8,128,512]{2,1,0:T(8,128)(2,1)}), bf16[8,128,512]{2,1,0:T(8,128)(2,1)}, u32[]{:S(2)}, u32[]{:S(2)}) async-start(bf16[8,128,512]{2,1,0:T(8,128)(2,1)} %bitcast.6), calls=%async_computation | async-start | bytes 2097152 | tf_op jit(solution)/shard_map/all_to_all | solution.py:392
  11.6 7.5 %shard_map.59 = (bf16[1024,1024]{1,0:T(8,128)(2,1)S(1)}, bf16[128,1024]{1,0:T(8,128)(2,1)}, bf16[128,1024]{1,0:T(8,128)(2,1)}, bf16[128,1024]{1,0:T(8,128)(2,1)}...) custom-call(bf16[1024,2048]{1,0:T(8,128)(2,1)} %bitcast.8, ...), custom_call_target="tpu_custom_call" | custom-call | flops 1 | bytes 1 | tf_op jit(solution)/shard_map/pallas_call | solution.py:147
  19.1 0.7 %collective-permute-start.1 = (bf16[128,1024]{1,0:T(8,128)(2,1)}, bf16[128,1024]{1,0:T(8,128)(2,1)S(1)}, u32[]{:S(2)}, u32[]{:S(2)}) collective-permute-start(bf16[128,1024]{1,0:T(8,128)(2,1)} %get-tuple-element.20), channel_id=1, source_target_pairs={{28,24},{29,25},{30,26},{31,27}} | collective-permute-start | bytes 786440 | tf_op jit(solution)/shard_map/ppermute | solution.py:389
  19.7 1.4 %collective-permute-start.3 = (bf16[128,1024]{1,0:T(8,128)(2,1)}, bf16[128,1024]{1,0:T(8,128)(2,1)}, u32[]{:S(2)}, u32[]{:S(2)}) collective-permute-start(bf16[128,1024]{1,0:T(8,128)(2,1)} %get-tuple-element.23), channel_id=1, source_target_pairs={{28,4},{29,5},{30,6},{31,7}} | collective-permute-start | bytes 786440 | tf_op jit(solution)/shard_map/ppermute | solution.py:389
  21.1 1.4 %collective-permute-start.5 = (bf16[128,1024]{1,0:T(8,128)(2,1)}, bf16[128,1024]{1,0:T(8,128)(2,1)}, u32[]{:S(2)}, u32[]{:S(2)}) collective-permute-start(bf16[128,1024]{1,0:T(8,128)(2,1)} %get-tuple-element.26), channel_id=1, source_target_pairs={{28,24},{29,25},{30,26},{31,27}} | collective-permute-start | bytes 786440 | tf_op jit(solution)/shard_map/ppermute | solution.py:389
  22.5 1.4 %collective-permute-start.4 = (bf16[128,1024]{1,0:T(8,128)(2,1)}, bf16[128,1024]{1,0:T(8,128)(2,1)}, u32[]{:S(2)}, u32[]{:S(2)}) collective-permute-start(bf16[128,1024]{1,0:T(8,128)(2,1)} %get-tuple-element.24), channel_id=1, source_target_pairs={{28,24},{29,17},{30,26},{31,19}} | collective-permute-start | bytes 786440 | tf_op jit(solution)/shard_map/ppermute | solution.py:389
  23.9 0.0 collective-permute-start
  23.9 4.4 %shard_map.61 = (bf16[1024,1024]{1,0:T(8,128)(2,1)}, bf16[16,128]{1,0:T(8,128)(2,1)S(1)}) custom-call(s32[1]{0:T(128)} %bitcast.first_ref, bf16[1024,1024]{1,0:T(8,128)(2,1)S(1)} %get-tuple-element.15.q_ref.refs_0_, bf16[1024,512]{1,0:T(8,128)(2,1)S(1)} %copy-done), custom_call_target="tpu_custom_call" | custom-call | flops 1 | bytes 1 | tf_op jit(solution)/shard_map/pallas_call | solution.py:296
  28.3 0.7 %shard_map.62.refs_1_ = bf16[128,1024]{1,0:T(8,128)(2,1)} custom-call(s32[1]{0:T(128)} %bitcast.2.which_ref, bf16[128,1024]{1,0:T(8,128)(2,1)} %get-tuple-element.19.a_hbm, bf16[128,1024]{1,0:T(8,128)(2,1)S(1)} %collective-permute-done.1.b_hbm, bf16[16,128]{1,0:T(8,128)(2,1)S(1)} %get-tuple-element.21.refs_0_), custom_call_target="tpu_custom_call" | custom-call | flops 1 | bytes 1 | tf_op jit(solution)/shard_map/pallas_call | solution.py:217
  29.0 0.7 %collective-permute-start.2 = (bf16[128,1024]{1,0:T(8,128)(2,1)}, bf16[128,1024]{1,0:T(8,128)(2,1)S(1)}, u32[]{:S(2)}, u32[]{:S(2)}) collective-permute-start(bf16[128,1024]{1,0:T(8,128)(2,1)} %shard_map.62.refs_1_), channel_id=1, source_target_pairs={{24,0},{28,12},{25,1},{29,13},{26,2},{30,14},{27,3},{31,15}} | collective-permute-start | bytes 786440 | tf_op jit(solution)/shard_map/ppermute | solution.py:389
  29.7 0.0 collective-permute-done.3.refs_1_
  29.7 1.4 %collective-permute-start.7 = (bf16[128,1024]{1,0:T(8,128)(2,1)}, bf16[128,1024]{1,0:T(8,128)(2,1)}, u32[]{:S(2)}, u32[]{:S(2)}) collective-permute-start(bf16[128,1024]{1,0:T(8,128)(2,1)} %shard_map.65), channel_id=1, source_target_pairs={{28,24},{29,25},{30,26},{31,27}} | collective-permute-start | bytes 786440 | tf_op jit(solution)/shard_map/ppermute | solution.py:389
  31.1 0.0 collective-permute-done.5.b_hbm
  31.1 1.6 %shard_map.64 = bf16[128,1024]{1,0:T(8,128)(2,1)} custom-call(s32[1]{0:T(128)} %bitcast.2.which_ref, bf16[128,1024]{1,0:T(8,128)(2,1)} %get-tuple-element.25.a_hbm, bf16[128,1024]{1,0:T(8,128)(2,1)} %collective-permute-done.5.b_hbm, bf16[16,128]{1,0:T(8,128)(2,1)S(1)} %get-tuple-element.21.refs_0_, bf16[128,1024]{1,0:T(8,128)(2,1)} %collective-permute-done.3.refs_1_), custom_call_target="tpu_custom_call" | custom-call | flops 1 | bytes 1 | tf_op jit(solution)/shard_map/pallas_call | solution.py:217
  32.8 1.4 %collective-permute-start.6 = (bf16[128,1024]{1,0:T(8,128)(2,1)}, bf16[128,1024]{1,0:T(8,128)(2,1)}, u32[]{:S(2)}, u32[]{:S(2)}) collective-permute-start(bf16[128,1024]{1,0:T(8,128)(2,1)} %shard_map.64), channel_id=1, source_target_pairs={{24,8},{28,20},{25,9},{29,21},{26,10},{30,22},{27,11},{31,23}} | collective-permute-start | bytes 786440 | tf_op jit(solution)/shard_map/ppermute | solution.py:389
  34.1 0.0 collective-permute-done.4.refs_2_
  34.1 1.3 %collective-permute-start.8 = (bf16[128,1024]{1,0:T(8,128)(2,1)}, bf16[128,1024]{1,0:T(8,128)(2,1)}, u32[]{:S(2)}, u32[]{:S(2)}) collective-permute-start(bf16[128,1024]{1,0:T(8,128)(2,1)} %collective-permute-done.4.refs_2_), channel_id=1, source_target_pairs={{24,16},{26,18}} | collective-permute-start | bytes 786440 | tf_op jit(solution)/shard_map/ppermute | solution.py:389
  35.5 0.0 collective-permute-done.2.refs_2_.refs_3_
  35.5 4.6 %shard_map.63 = (bf16[1024,1024]{1,0:T(8,128)(2,1)}, bf16[16,128]{1,0:T(8,128)(2,1)}) custom-call(s32[1]{0:T(128)} %bitcast.first_ref, bf16[1024,1024]{1,0:T(8,128)(2,1)S(1)} %get-tuple-element.15.q_ref.refs_0_, bf16[1024,512]{1,0:T(8,128)(2,1)S(1)} %copy-done, bf16[256,512]{1,0:T(8,128)(2,1)} %collective-permute-done.refs_0_, ...), custom_call_target="tpu_custom_call", output_to_operand_aliasing={{0}: (4, {})} | custom-call | flops 1000000000 | bytes 1 | tf_op jit(solution)/shard_map/pallas_call | solution.py:296
  40.1 0.0 collective-permute-done.7.refs_5_
  40.1 0.0 collective-permute-done.6.refs_4_
  40.2 11.5 %collective-permute-done.8.refs_6_ = bf16[128,1024]{1,0:T(8,128)(2,1)} collective-permute-done((bf16[128,1024]{1,0:T(8,128)(2,1)}, bf16[128,1024]{1,0:T(8,128)(2,1)}, u32[]{:S(2)}, u32[]{:S(2)}) %collective-permute-start.8) | collective-permute-done | bytes 262176 | tf_op jit(solution)/shard_map/ppermute | solution.py:389
  51.7 3.5 %shard_map.66 = bf16[128,1024]{1,0:T(8,128)(2,1)} custom-call(s32[1]{0:T(128)} %bitcast.4.which_ref, bf16[1024,1024]{1,0:T(8,128)(2,1)S(1)} %get-tuple-element.15.q_ref.refs_0_, bf16[128,1024]{1,0:T(8,128)(2,1)} %collective-permute-done.3.refs_1_, bf16[128,1024]{1,0:T(8,128)(2,1)} %collective-permute-done.4.refs_2_, ...), custom_call_target="tpu_custom_call" | custom-call | flops 1 | bytes 1 | tf_op jit(solution)/shard_map/pallas_call | solution.py:351
  (6 shorter events, 0.0 us)
Async XLA Ops:
  5.4 46.3 %all-to-all-start = ((bf16[8,128,512]{2,1,0:T(8,128)(2,1)}), bf16[8,128,512]{2,1,0:T(8,128)(2,1)}, u32[]{:S(2)}, u32[]{:S(2)}) async-start(bf16[8,128,512]{2,1,0:T(8,128)(2,1)} %bitcast.6), calls=%async_computation | async-start | bytes 2097152 | tf_op jit(solution)/shard_map/all_to_all | solution.py:392
  11.6 12.3 %copy-start = (bf16[1024,512]{1,0:T(8,128)(2,1)S(1)}, bf16[1024,512]{1,0:T(8,128)(2,1)}, u32[]{:S(2)}) copy-start(bf16[1024,512]{1,0:T(8,128)(2,1)} %get-tuple-element.16.kv_ref) | copy-start | bytes 3145732
  19.1 9.2 %collective-permute-start.1 = (bf16[128,1024]{1,0:T(8,128)(2,1)}, bf16[128,1024]{1,0:T(8,128)(2,1)S(1)}, u32[]{:S(2)}, u32[]{:S(2)}) collective-permute-start(bf16[128,1024]{1,0:T(8,128)(2,1)} %get-tuple-element.20), channel_id=1, source_target_pairs={{28,24},{29,25},{30,26},{31,27}} | collective-permute-start | bytes 786440 | tf_op jit(solution)/shard_map/ppermute | solution.py:389
  19.7 10.0 %collective-permute-start.3 = (bf16[128,1024]{1,0:T(8,128)(2,1)}, bf16[128,1024]{1,0:T(8,128)(2,1)}, u32[]{:S(2)}, u32[]{:S(2)}) collective-permute-start(bf16[128,1024]{1,0:T(8,128)(2,1)} %get-tuple-element.23), channel_id=1, source_target_pairs={{28,4},{29,5},{30,6},{31,7}} | collective-permute-start | bytes 786440 | tf_op jit(solution)/shard_map/ppermute | solution.py:389
  21.1 10.0 %collective-permute-start.5 = (bf16[128,1024]{1,0:T(8,128)(2,1)}, bf16[128,1024]{1,0:T(8,128)(2,1)}, u32[]{:S(2)}, u32[]{:S(2)}) collective-permute-start(bf16[128,1024]{1,0:T(8,128)(2,1)} %get-tuple-element.26), channel_id=1, source_target_pairs={{28,24},{29,25},{30,26},{31,27}} | collective-permute-start | bytes 786440 | tf_op jit(solution)/shard_map/ppermute | solution.py:389
  22.5 11.7 %collective-permute-start.4 = (bf16[128,1024]{1,0:T(8,128)(2,1)}, bf16[128,1024]{1,0:T(8,128)(2,1)}, u32[]{:S(2)}, u32[]{:S(2)}) collective-permute-start(bf16[128,1024]{1,0:T(8,128)(2,1)} %get-tuple-element.24), channel_id=1, source_target_pairs={{28,24},{29,17},{30,26},{31,19}} | collective-permute-start | bytes 786440 | tf_op jit(solution)/shard_map/ppermute | solution.py:389
  23.9 11.7 %collective-permute-start = (bf16[256,512]{1,0:T(8,128)(2,1)}, bf16[256,512]{1,0:T(8,128)(2,1)}, u32[]{:S(2)}, u32[]{:S(2)}) collective-permute-start(bf16[256,512]{1,0:T(8,128)(2,1)} %get-tuple-element.17), channel_id=1, source_target_pairs={{0,1},{1,2},{2,3},{3,0},{4,5},{5,6},{6,7},{7,4},{8,9},{9,10},{10,1... | collective-permute-start | bytes 786440 | tf_op jit(solution)/shard_map/ppermute | solution.py:393
  29.0 6.5 %collective-permute-start.2 = (bf16[128,1024]{1,0:T(8,128)(2,1)}, bf16[128,1024]{1,0:T(8,128)(2,1)S(1)}, u32[]{:S(2)}, u32[]{:S(2)}) collective-permute-start(bf16[128,1024]{1,0:T(8,128)(2,1)} %shard_map.62.refs_1_), channel_id=1, source_target_pairs={{24,0},{28,12},{25,1},{29,13},{26,2},{30,14},{27,3},{31,15}} | collective-permute-start | bytes 786440 | tf_op jit(solution)/shard_map/ppermute | solution.py:389
  29.7 10.4 %collective-permute-start.7 = (bf16[128,1024]{1,0:T(8,128)(2,1)}, bf16[128,1024]{1,0:T(8,128)(2,1)}, u32[]{:S(2)}, u32[]{:S(2)}) collective-permute-start(bf16[128,1024]{1,0:T(8,128)(2,1)} %shard_map.65), channel_id=1, source_target_pairs={{28,24},{29,25},{30,26},{31,27}} | collective-permute-start | bytes 786440 | tf_op jit(solution)/shard_map/ppermute | solution.py:389
  32.8 7.4 %collective-permute-start.6 = (bf16[128,1024]{1,0:T(8,128)(2,1)}, bf16[128,1024]{1,0:T(8,128)(2,1)}, u32[]{:S(2)}, u32[]{:S(2)}) collective-permute-start(bf16[128,1024]{1,0:T(8,128)(2,1)} %shard_map.64), channel_id=1, source_target_pairs={{24,8},{28,20},{25,9},{29,21},{26,10},{30,22},{27,11},{31,23}} | collective-permute-start | bytes 786440 | tf_op jit(solution)/shard_map/ppermute | solution.py:389
  34.1 17.5 %collective-permute-start.8 = (bf16[128,1024]{1,0:T(8,128)(2,1)}, bf16[128,1024]{1,0:T(8,128)(2,1)}, u32[]{:S(2)}, u32[]{:S(2)}) collective-permute-start(bf16[128,1024]{1,0:T(8,128)(2,1)} %collective-permute-done.4.refs_2_), channel_id=1, source_target_pairs={{24,16},{26,18}} | collective-permute-start | bytes 786440 | tf_op jit(solution)/shard_map/ppermute | solution.py:389

commit v6 on v5

--- a/solution.py
+++ b/solution.py
@@ -159,32 +159,6 @@
         compiler_params=params(20),
         cost_estimate=cost(),
     )(*in_hbm(rows, weight))
-
-
-def nothing_kernel(*refs):
-    pass
-
-
-def once(block, arrays):
-    return pl.pallas_call(
-        nothing_kernel,
-        out_shape=hbm_array(*block.shape),
-        in_specs=[HBM] + [ANY] * len(arrays),
-        out_specs=HBM,
-        input_output_aliases={0: 0},
-        cost_estimate=cost(),
-    )(*in_hbm(block), *arrays)
-
-
-def choose_kernel(which_ref, a_hbm, b_hbm, *refs):
-    out_ref, sem = refs[-2:]
-    for flag, source in ((1, a_hbm), (0, b_hbm)):
-
-        @pl.when(which_ref[0] == flag)
-        def _(source=source):
-            pltpu.make_async_copy(source, out_ref, sem).start()
-
-    pltpu.make_async_copy(b_hbm, out_ref, sem).wait()
 
 
 def nothing_kernel(*refs):

time: 55.5 us -> 55.5 us (level)
  no operation moved by 1% of the time
where the time goes in v6:
time: 55.5 us; the launch traced here: 55.2 us
  Pallas kernels  27.1 us (49%)
  starting transfers between devices  15.7 us (28%)
  waiting for transfers between devices  11.6 us (21%)
  between operations  0.86 us (2%)
    ppermute x8, waiting for transfers between devices, send(): return lax.ppermute(block, ('depth', 'tok'), pairs)  11.5 us
    ppermute x8, starting transfers between devices, send(): return lax.ppermute(block, ('depth', 'tok'), pairs)  9.52 us
    pallas_call x2, Pallas kernels, band_attend(): pl.pallas_call(functools.partial(band_kernel, blocks_of), out_shape=[arra...  8.96 us
    pallas_call x1, Pallas kernels, project_q(): pl.pallas_call(functools.partial(project_q_kernel, part), out_shape=[arra...  7.48 us
    all_to_all x1, starting transfers between devices, body(): lax.all_to_all(kv.reshape(steps, part, kv.shape[1]), 'depth', split_axis=...  6.15 us
    pallas_call x1, Pallas kernels, project_kv(): pl.pallas_call(project_kv_kernel, out_shape=[hbm_array(count, 2 * width),...  4.78 us
    pallas_call x1, Pallas kernels, depth_attend(): pl.pallas_call(functools.partial(depth_kernel, 1 + len(queries)), out_sha...  3.46 us
    pallas_call x2, Pallas kernels, choose(): pl.pallas_call(choose_kernel, out_shape=buffer(*a.shape), in_specs=[SMEM,...  2.38 us
  transfers between devices with their start and end apart: 10, of which 1 were waited for; matrix products, arithmetic and copies ran while one was open for 0% of the time, Pallas kernels for 34%

profile of v6, /device:TPU:16, one launch (start us, length us, event | category | flops | bytes accessed | tf_op | source)
XLA Modules:
  0.0 55.2 jit_solution(968450836448906631)
XLA Ops:
  0.6 4.8 %shard_map.60 = (bf16[1024,512]{1,0:T(8,128)(2,1)}, bf16[256,512]{1,0:T(8,128)(2,1)}) custom-call(bf16[1024,2048]{1,0:T(8,128)(2,1)} %bitcast.7, bf16[2048,256]{1,0:T(8,128)(2,1)} %wk_hbm.1, bf16[2048,256]{1,0:T(8,128)(2,1)} %wv_hbm.1), custom_call_target="tpu_custom_call" | custom-call | flops 1 | bytes 1 | tf_op jit(solution)/shard_map/pallas_call | solution.py:108
  5.4 6.1 %all-to-all-start = ((bf16[8,128,512]{2,1,0:T(8,128)(2,1)}), bf16[8,128,512]{2,1,0:T(8,128)(2,1)}, u32[]{:S(2)}, u32[]{:S(2)}) async-start(bf16[8,128,512]{2,1,0:T(8,128)(2,1)} %bitcast.6), calls=%async_computation | async-start | bytes 2097152 | tf_op jit(solution)/shard_map/all_to_all | solution.py:366
  11.6 7.5 %shard_map.59 = (bf16[1024,1024]{1,0:T(8,128)(2,1)S(1)}, bf16[128,1024]{1,0:T(8,128)(2,1)}, bf16[128,1024]{1,0:T(8,128)(2,1)}, bf16[128,1024]{1,0:T(8,128)(2,1)}...) custom-call(bf16[1024,2048]{1,0:T(8,128)(2,1)} %bitcast.8, ...), custom_call_target="tpu_custom_call" | custom-call | flops 1 | bytes 1 | tf_op jit(solution)/shard_map/pallas_call | solution.py:147
  19.1 0.7 %collective-permute-start.1 = (bf16[128,1024]{1,0:T(8,128)(2,1)}, bf16[128,1024]{1,0:T(8,128)(2,1)S(1)}, u32[]{:S(2)}, u32[]{:S(2)}) collective-permute-start(bf16[128,1024]{1,0:T(8,128)(2,1)} %get-tuple-element.20), channel_id=1, source_target_pairs={{28,24},{29,25},{30,26},{31,27}} | collective-permute-start | bytes 786440 | tf_op jit(solution)/shard_map/ppermute | solution.py:363
  19.7 1.4 %collective-permute-start.3 = (bf16[128,1024]{1,0:T(8,128)(2,1)}, bf16[128,1024]{1,0:T(8,128)(2,1)}, u32[]{:S(2)}, u32[]{:S(2)}) collective-permute-start(bf16[128,1024]{1,0:T(8,128)(2,1)} %get-tuple-element.23), channel_id=1, source_target_pairs={{28,4},{29,5},{30,6},{31,7}} | collective-permute-start | bytes 786440 | tf_op jit(solution)/shard_map/ppermute | solution.py:363
  21.1 1.4 %collective-permute-start.5 = (bf16[128,1024]{1,0:T(8,128)(2,1)}, bf16[128,1024]{1,0:T(8,128)(2,1)}, u32[]{:S(2)}, u32[]{:S(2)}) collective-permute-start(bf16[128,1024]{1,0:T(8,128)(2,1)} %get-tuple-element.26), channel_id=1, source_target_pairs={{28,24},{29,25},{30,26},{31,27}} | collective-permute-start | bytes 786440 | tf_op jit(solution)/shard_map/ppermute | solution.py:363
  22.5 1.4 %collective-permute-start.4 = (bf16[128,1024]{1,0:T(8,128)(2,1)}, bf16[128,1024]{1,0:T(8,128)(2,1)}, u32[]{:S(2)}, u32[]{:S(2)}) collective-permute-start(bf16[128,1024]{1,0:T(8,128)(2,1)} %get-tuple-element.24), channel_id=1, source_target_pairs={{28,24},{29,17},{30,26},{31,19}} | collective-permute-start | bytes 786440 | tf_op jit(solution)/shard_map/ppermute | solution.py:363
  23.9 0.0 collective-permute-start
  23.9 4.4 %shard_map.61 = (bf16[1024,1024]{1,0:T(8,128)(2,1)}, bf16[16,128]{1,0:T(8,128)(2,1)S(1)}) custom-call(s32[1]{0:T(128)} %bitcast.first_ref, bf16[1024,1024]{1,0:T(8,128)(2,1)S(1)} %get-tuple-element.15.q_ref.refs_0_, bf16[1024,512]{1,0:T(8,128)(2,1)S(1)} %copy-done), custom_call_target="tpu_custom_call" | custom-call | flops 1 | bytes 1 | tf_op jit(solution)/shard_map/pallas_call | solution.py:270
  28.3 0.7 %shard_map.62.refs_1_ = bf16[128,1024]{1,0:T(8,128)(2,1)} custom-call(s32[1]{0:T(128)} %bitcast.2.which_ref, bf16[128,1024]{1,0:T(8,128)(2,1)} %get-tuple-element.19.a_hbm, bf16[128,1024]{1,0:T(8,128)(2,1)S(1)} %collective-permute-done.1.b_hbm, bf16[16,128]{1,0:T(8,128)(2,1)S(1)} %get-tuple-element.21.refs_0_), custom_call_target="tpu_custom_call" | custom-call | flops 1 | bytes 1 | tf_op jit(solution)/shard_map/pallas_call | solution.py:191
  29.0 0.7 %collective-permute-start.2 = (bf16[128,1024]{1,0:T(8,128)(2,1)}, bf16[128,1024]{1,0:T(8,128)(2,1)S(1)}, u32[]{:S(2)}, u32[]{:S(2)}) collective-permute-start(bf16[128,1024]{1,0:T(8,128)(2,1)} %shard_map.62.refs_1_), channel_id=1, source_target_pairs={{24,0},{28,12},{25,1},{29,13},{26,2},{30,14},{27,3},{31,15}} | collective-permute-start | bytes 786440 | tf_op jit(solution)/shard_map/ppermute | solution.py:363
  29.7 0.0 collective-permute-done.3.refs_1_
  29.7 1.4 %collective-permute-start.7 = (bf16[128,1024]{1,0:T(8,128)(2,1)}, bf16[128,1024]{1,0:T(8,128)(2,1)}, u32[]{:S(2)}, u32[]{:S(2)}) collective-permute-start(bf16[128,1024]{1,0:T(8,128)(2,1)} %shard_map.65), channel_id=1, source_target_pairs={{28,24},{29,25},{30,26},{31,27}} | collective-permute-start | bytes 786440 | tf_op jit(solution)/shard_map/ppermute | solution.py:363
  31.1 0.0 collective-permute-done.5.b_hbm
  31.1 1.6 %shard_map.64 = bf16[128,1024]{1,0:T(8,128)(2,1)} custom-call(s32[1]{0:T(128)} %bitcast.2.which_ref, bf16[128,1024]{1,0:T(8,128)(2,1)} %get-tuple-element.25.a_hbm, bf16[128,1024]{1,0:T(8,128)(2,1)} %collective-permute-done.5.b_hbm, bf16[16,128]{1,0:T(8,128)(2,1)S(1)} %get-tuple-element.21.refs_0_, bf16[128,1024]{1,0:T(8,128)(2,1)} %collective-permute-done.3.refs_1_), custom_call_target="tpu_custom_call" | custom-call | flops 1 | bytes 1 | tf_op jit(solution)/shard_map/pallas_call | solution.py:191
  32.8 1.4 %collective-permute-start.6 = (bf16[128,1024]{1,0:T(8,128)(2,1)}, bf16[128,1024]{1,0:T(8,128)(2,1)}, u32[]{:S(2)}, u32[]{:S(2)}) collective-permute-start(bf16[128,1024]{1,0:T(8,128)(2,1)} %shard_map.64), channel_id=1, source_target_pairs={{24,8},{28,20},{25,9},{29,21},{26,10},{30,22},{27,11},{31,23}} | collective-permute-start | bytes 786440 | tf_op jit(solution)/shard_map/ppermute | solution.py:363
  34.1 0.0 collective-permute-done.4.refs_2_
  34.1 1.3 %collective-permute-start.8 = (bf16[128,1024]{1,0:T(8,128)(2,1)}, bf16[128,1024]{1,0:T(8,128)(2,1)}, u32[]{:S(2)}, u32[]{:S(2)}) collective-permute-start(bf16[128,1024]{1,0:T(8,128)(2,1)} %collective-permute-done.4.refs_2_), channel_id=1, source_target_pairs={{24,16},{26,18}} | collective-permute-start | bytes 786440 | tf_op jit(solution)/shard_map/ppermute | solution.py:363
  35.5 0.0 collective-permute-done.2.refs_2_.refs_3_
  35.5 4.6 %shard_map.63 = (bf16[1024,1024]{1,0:T(8,128)(2,1)}, bf16[16,128]{1,0:T(8,128)(2,1)}) custom-call(s32[1]{0:T(128)} %bitcast.first_ref, bf16[1024,1024]{1,0:T(8,128)(2,1)S(1)} %get-tuple-element.15.q_ref.refs_0_, bf16[1024,512]{1,0:T(8,128)(2,1)S(1)} %copy-done, bf16[256,512]{1,0:T(8,128)(2,1)} %collective-permute-done.refs_0_, ...), custom_call_target="tpu_custom_call", output_to_operand_aliasing={{0}: (4, {})} | custom-call | flops 1000000000 | bytes 1 | tf_op jit(solution)/shard_map/pallas_call | solution.py:270
  40.1 0.0 collective-permute-done.7.refs_5_
  40.1 0.0 collective-permute-done.6.refs_4_
  40.2 11.5 %collective-permute-done.8.refs_6_ = bf16[128,1024]{1,0:T(8,128)(2,1)} collective-permute-done((bf16[128,1024]{1,0:T(8,128)(2,1)}, bf16[128,1024]{1,0:T(8,128)(2,1)}, u32[]{:S(2)}, u32[]{:S(2)}) %collective-permute-start.8) | collective-permute-done | bytes 262176 | tf_op jit(solution)/shard_map/ppermute | solution.py:363
  51.7 3.5 %shard_map.66 = bf16[128,1024]{1,0:T(8,128)(2,1)} custom-call(s32[1]{0:T(128)} %bitcast.4.which_ref, bf16[1024,1024]{1,0:T(8,128)(2,1)S(1)} %get-tuple-element.15.q_ref.refs_0_, bf16[128,1024]{1,0:T(8,128)(2,1)} %collective-permute-done.3.refs_1_, bf16[128,1024]{1,0:T(8,128)(2,1)} %collective-permute-done.4.refs_2_, ...), custom_call_target="tpu_custom_call" | custom-call | flops 1 | bytes 1 | tf_op jit(solution)/shard_map/pallas_call | solution.py:325
  (6 shorter events, 0.0 us)
Async XLA Ops:
  5.4 46.3 %all-to-all-start = ((bf16[8,128,512]{2,1,0:T(8,128)(2,1)}), bf16[8,128,512]{2,1,0:T(8,128)(2,1)}, u32[]{:S(2)}, u32[]{:S(2)}) async-start(bf16[8,128,512]{2,1,0:T(8,128)(2,1)} %bitcast.6), calls=%async_computation | async-start | bytes 2097152 | tf_op jit(solution)/shard_map/all_to_all | solution.py:366
  11.6 12.3 %copy-start = (bf16[1024,512]{1,0:T(8,128)(2,1)S(1)}, bf16[1024,512]{1,0:T(8,128)(2,1)}, u32[]{:S(2)}) copy-start(bf16[1024,512]{1,0:T(8,128)(2,1)} %get-tuple-element.16.kv_ref) | copy-start | bytes 3145732
  19.1 9.2 %collective-permute-start.1 = (bf16[128,1024]{1,0:T(8,128)(2,1)}, bf16[128,1024]{1,0:T(8,128)(2,1)S(1)}, u32[]{:S(2)}, u32[]{:S(2)}) collective-permute-start(bf16[128,1024]{1,0:T(8,128)(2,1)} %get-tuple-element.20), channel_id=1, source_target_pairs={{28,24},{29,25},{30,26},{31,27}} | collective-permute-start | bytes 786440 | tf_op jit(solution)/shard_map/ppermute | solution.py:363
  19.7 10.0 %collective-permute-start.3 = (bf16[128,1024]{1,0:T(8,128)(2,1)}, bf16[128,1024]{1,0:T(8,128)(2,1)}, u32[]{:S(2)}, u32[]{:S(2)}) collective-permute-start(bf16[128,1024]{1,0:T(8,128)(2,1)} %get-tuple-element.23), channel_id=1, source_target_pairs={{28,4},{29,5},{30,6},{31,7}} | collective-permute-start | bytes 786440 | tf_op jit(solution)/shard_map/ppermute | solution.py:363
  21.1 10.0 %collective-permute-start.5 = (bf16[128,1024]{1,0:T(8,128)(2,1)}, bf16[128,1024]{1,0:T(8,128)(2,1)}, u32[]{:S(2)}, u32[]{:S(2)}) collective-permute-start(bf16[128,1024]{1,0:T(8,128)(2,1)} %get-tuple-element.26), channel_id=1, source_target_pairs={{28,24},{29,25},{30,26},{31,27}} | collective-permute-start | bytes 786440 | tf_op jit(solution)/shard_map/ppermute | solution.py:363
  22.5 11.7 %collective-permute-start.4 = (bf16[128,1024]{1,0:T(8,128)(2,1)}, bf16[128,1024]{1,0:T(8,128)(2,1)}, u32[]{:S(2)}, u32[]{:S(2)}) collective-permute-start(bf16[128,1024]{1,0:T(8,128)(2,1)} %get-tuple-element.24), channel_id=1, source_target_pairs={{28,24},{29,17},{30,26},{31,19}} | collective-permute-start | bytes 786440 | tf_op jit(solution)/shard_map/ppermute | solution.py:363
  23.9 11.7 %collective-permute-start = (bf16[256,512]{1,0:T(8,128)(2,1)}, bf16[256,512]{1,0:T(8,128)(2,1)}, u32[]{:S(2)}, u32[]{:S(2)}) collective-permute-start(bf16[256,512]{1,0:T(8,128)(2,1)} %get-tuple-element.17), channel_id=1, source_target_pairs={{0,1},{1,2},{2,3},{3,0},{4,5},{5,6},{6,7},{7,4},{8,9},{9,10},{10,1... | collective-permute-start | bytes 786440 | tf_op jit(solution)/shard_map/ppermute | solution.py:367
  29.0 6.5 %collective-permute-start.2 = (bf16[128,1024]{1,0:T(8,128)(2,1)}, bf16[128,1024]{1,0:T(8,128)(2,1)S(1)}, u32[]{:S(2)}, u32[]{:S(2)}) collective-permute-start(bf16[128,1024]{1,0:T(8,128)(2,1)} %shard_map.62.refs_1_), channel_id=1, source_target_pairs={{24,0},{28,12},{25,1},{29,13},{26,2},{30,14},{27,3},{31,15}} | collective-permute-start | bytes 786440 | tf_op jit(solution)/shard_map/ppermute | solution.py:363
  29.7 10.4 %collective-permute-start.7 = (bf16[128,1024]{1,0:T(8,128)(2,1)}, bf16[128,1024]{1,0:T(8,128)(2,1)}, u32[]{:S(2)}, u32[]{:S(2)}) collective-permute-start(bf16[128,1024]{1,0:T(8,128)(2,1)} %shard_map.65), channel_id=1, source_target_pairs={{28,24},{29,25},{30,26},{31,27}} | collective-permute-start | bytes 786440 | tf_op jit(solution)/shard_map/ppermute | solution.py:363
  32.8 7.4 %collective-permute-start.6 = (bf16[128,1024]{1,0:T(8,128)(2,1)}, bf16[128,1024]{1,0:T(8,128)(2,1)}, u32[]{:S(2)}, u32[]{:S(2)}) collective-permute-start(bf16[128,1024]{1,0:T(8,128)(2,1)} %shard_map.64), channel_id=1, source_target_pairs={{24,8},{28,20},{25,9},{29,21},{26,10},{30,22},{27,11},{31,23}} | collective-permute-start | bytes 786440 | tf_op jit(solution)/shard_map/ppermute | solution.py:363
  34.1 17.5 %collective-permute-start.8 = (bf16[128,1024]{1,0:T(8,128)(2,1)}, bf16[128,1024]{1,0:T(8,128)(2,1)}, u32[]{:S(2)}, u32[]{:S(2)}) collective-permute-start(bf16[128,1024]{1,0:T(8,128)(2,1)} %collective-permute-done.4.refs_2_), channel_id=1, source_target_pairs={{24,16},{26,18}} | collective-permute-start | bytes 786440 | tf_op jit(solution)/shard_map/ppermute | solution.py:363
